TPU v7x, 256 devices: a whole 4x4x8 slice. The times are simulated.
256 devices in a mesh: seq: 64 (over y, z, x_hi), head: 4 (over x_lo, core).
Axes of the slice: x: 4 (x_hi: 2, x_lo: 2; x = x_hi * 2 + x_lo), y: 4, z: 8, core: 2. Of those that a mesh axis runs over, the one named last changes fastest.
Arguments:
- hidden_in: bfloat16 [12288, 2048], P('seq', 'head'), may hold values from -6 to 6
- delta_q: bfloat16 [12288, 2048], P('seq', 'head'), may hold values from -6 to 6
- delta_k: bfloat16 [12288, 2048], P('seq', 'head'), may hold values from -6 to 6
- delta_v: bfloat16 [12288, 2048], P('seq', 'head'), may hold values from -6 to 6
- beta: float32 [12288, 16], P('seq', 'head'), may hold values from 0.002 to 0.02
- log_decay: float32 [12288, 16], P('seq', 'head'), may hold values from -1 to 0
- resets: int32 [12288], P('seq'), may hold values from 0 to 1, as said below
- attn_q: bfloat16 [12288, 2048], P('seq', 'head'), may hold values from -5.5 to 5.5
- attn_k: bfloat16 [12288, 2048], P('seq', 'head'), may hold values from -5.5 to 5.5
- attn_v: bfloat16 [12288, 2048], P('seq', 'head'), may hold values from -6 to 6
- delta_gain: float32 [128], replicated, may hold values from 0.5 to 1.5
- attn_gain: float32 [128], replicated, may hold values from 0.5 to 1.5
- out_weight: bfloat16 [2048, 2048], P('head'), may hold values from -0.125 to 0.125
Outputs:
- mixed: bfloat16 [12288, 2048], P('seq', 'head')
Inputs may be any that keep to these rules, and one draw needn't show every extreme that they name: `resets`: exactly three ones, one in each of the first three runs of 4096 tokens, never at the first token of a run.
All inputs are finite; a program needn't handle non-finite values.
Results may differ from a plain program's by a relative error of at most 0.013.
Values may be sent and summed in bfloat16 or wider, within the bound.
A program may use at most 256 MiB of HBM per device.

v0:
```python
import jax
import jax.numpy as jnp
from jax import lax
from jax.sharding import PartitionSpec as P

HEAD_DIM = 128
BLOCK = 64


HIGHEST_MODE = lax.Precision.HIGHEST
EPSILON = 1e-06


def prefix(array, axis, join, neutral):
    place = lax.axis_index(axis)
    gathered = jax.tree.map(
        lambda a, kind: lax.all_gather(a.astype(kind), axis), array, (jnp.bfloat16, jnp.bfloat16)
    )
    state = jax.tree.map(lambda a, e: jnp.zeros_like(a) + jnp.asarray(e, a.dtype), array, neutral)

    def one(hop, state):
        return join(
            state,
            jax.tree.map(
                lambda a, own: lax.dynamic_index_in_dim(a, hop, 0, False).astype(own.dtype),
                gathered,
                array,
            ),
        )

    return lax.fori_loop(0, place, one, state)


def unit_rows(tensor):
    return tensor * lax.rsqrt(jnp.sum(tensor * tensor, axis=-1, keepdims=True) + EPSILON)


def rms_scaled(tensor, scales):
    return tensor * lax.rsqrt(jnp.mean(tensor * tensor, axis=-1, keepdims=True) + EPSILON) * scales


def matmul_heads(left_side, right_side):
    return jnp.einsum("hij,hjk->hik", left_side, right_side, precision=HIGHEST_MODE)


def compose(earlier, later):
    first_a, first_b = earlier
    second_a, second_b = later
    return (matmul_heads(first_a, second_a), matmul_heads(first_b, second_a) + second_b)


def local(
    hidden_in,
    delta_q,
    delta_k,
    delta_v,
    beta,
    log_decay,
    resets,
    attn_q,
    attn_k,
    attn_v,
    delta_gain,
    attn_gain,
    out_weight,
):
    tokens = delta_q.shape[0]
    local_heads = delta_q.shape[1] // HEAD_DIM
    block_count = tokens // BLOCK
    position = lax.axis_index("seq")

    def blocked(tensor):
        return tensor.reshape(block_count, BLOCK, local_heads, HEAD_DIM).transpose(2, 0, 1, 3)

    query_block = blocked(
        unit_rows(delta_q.astype(jnp.float32).reshape(tokens, local_heads, HEAD_DIM))
        * HEAD_DIM ** (-0.5)
    )
    key_block = blocked(
        unit_rows(delta_k.astype(jnp.float32).reshape(tokens, local_heads, HEAD_DIM))
    )
    value_block = blocked(delta_v.astype(jnp.float32).reshape(tokens, local_heads, HEAD_DIM))
    decay_block = log_decay.reshape(block_count, BLOCK, local_heads).transpose(2, 0, 1)
    strength = beta.reshape(block_count, BLOCK, local_heads).transpose(2, 0, 1)
    reset_flags = resets.astype(jnp.float32).reshape(block_count, BLOCK)
    cumulative = jnp.cumsum(decay_block, axis=-1)
    counted = jnp.cumsum(reset_flags, axis=-1)
    reach_from = jnp.exp(cumulative) * (counted == 0.0)[None].astype(jnp.float32)
    index_row = jnp.arange(BLOCK)
    lower_part = index_row[:, None] >= index_row[None, :]
    strict = index_row[:, None] > index_row[None, :]
    same_doc = (counted[:, :, None] == counted[:, None, :]) & lower_part[None]
    log_gap = cumulative[..., :, None] - cumulative[..., None, :]
    ratios = jnp.where(same_doc[None], jnp.exp(jnp.minimum(log_gap, 0.0)), 0.0)
    key_inner = jnp.einsum("hnte,hnie->hnti", key_block, key_block, precision=HIGHEST_MODE)
    system = jnp.eye(BLOCK, dtype=jnp.float32) + strength[..., None] * jnp.where(
        strict, ratios * key_inner, 0.0
    )
    right_side = jnp.concatenate(
        [strength[..., None] * value_block, (strength * reach_from)[..., None] * key_block], axis=-1
    )
    solved = lax.linalg.triangular_solve(system, right_side, left_side=True, lower=True)
    new_values = solved[..., :HEAD_DIM]
    new_keys = solved[..., HEAD_DIM:]
    tail_keys = ratios[..., -1, :, None] * key_block
    identity = jnp.eye(HEAD_DIM, dtype=jnp.float32)
    block_a = reach_from[..., -1, None, None] * identity - jnp.einsum(
        "hnie,hnif->hnef", new_keys, tail_keys, precision=HIGHEST_MODE
    )
    block_b = jnp.einsum("hniv,hnif->hnvf", new_values, tail_keys, precision=HIGHEST_MODE)
    moved_a = jnp.moveaxis(block_a, 1, 0)
    moved_b = jnp.moveaxis(block_b, 1, 0)
    start_pair = (
        jnp.broadcast_to(identity, (local_heads, HEAD_DIM, HEAD_DIM)),
        jnp.zeros((local_heads, HEAD_DIM, HEAD_DIM), jnp.float32),
    )

    def fold_block(pair_ab, block_pair):
        return (compose(pair_ab, block_pair), None)

    (shard_a, shard_b), _ = lax.scan(fold_block, start_pair, (moved_a, moved_b))
    _, incoming = prefix((shard_a, shard_b), "seq", compose, start_pair)
    query_key = (
        jnp.einsum("hnte,hnie->hnti", query_block, key_block, precision=HIGHEST_MODE) * ratios
    )

    def emit_block(carried_state, inputs):
        query_rows, values_new, keys_new, reach_rows, weight_rows, trans_a, trans_b = inputs
        fresh_values = values_new - jnp.einsum(
            "hie,hve->hiv", keys_new, carried_state, precision=HIGHEST_MODE
        )
        carried = (
            jnp.einsum("hte,hve->htv", query_rows, carried_state, precision=HIGHEST_MODE)
            * reach_rows[..., None]
        )
        block_out = carried + jnp.einsum(
            "hti,hiv->htv", weight_rows, fresh_values, precision=HIGHEST_MODE
        )
        return (matmul_heads(carried_state, trans_a) + trans_b, block_out)

    scan_inputs = (
        jnp.moveaxis(query_block, 1, 0),
        jnp.moveaxis(new_values, 1, 0),
        jnp.moveaxis(new_keys, 1, 0),
        jnp.moveaxis(reach_from, 1, 0),
        jnp.moveaxis(query_key, 1, 0),
        moved_a,
        moved_b,
    )
    _, delta_raw = lax.scan(emit_block, incoming, scan_inputs)
    delta_raw = delta_raw.transpose(0, 2, 1, 3).reshape(tokens, local_heads, HEAD_DIM)
    delta_normed = rms_scaled(delta_raw, delta_gain)
    score_scale = HEAD_DIM ** (-0.5)
    query_heads = attn_q.reshape(tokens, local_heads, HEAD_DIM)
    query_pos = position * tokens + jnp.arange(tokens, dtype=jnp.int32)
    row_peak = jnp.full((local_heads, tokens), -1e30, jnp.float32)
    key_piece = lax.all_gather(attn_k, "seq", axis=0, tiled=True).reshape(-1, local_heads, HEAD_DIM)
    value_piece = lax.all_gather(attn_v, "seq", axis=0, tiled=True).reshape(
        -1, local_heads, HEAD_DIM
    )
    scores = (
        jnp.einsum("qhe,khe->hqk", query_heads, key_piece, preferred_element_type=jnp.float32)
        * score_scale
    )
    key_pos = jnp.arange(key_piece.shape[0], dtype=jnp.int32)
    visible = (key_pos[None, :] <= query_pos[:, None])[None]
    block_peak = jnp.max(jnp.where(visible, scores, -1e30), axis=-1)
    new_peak = jnp.maximum(row_peak, block_peak)
    weights = jnp.where(visible, jnp.exp(scores - new_peak[..., None]), 0.0)
    weight_sum = jnp.sum(weights, axis=-1)
    accumulated = jnp.einsum(
        "hqk,khe->hqe",
        weights.astype(jnp.bfloat16),
        value_piece,
        preferred_element_type=jnp.float32,
    )
    row_peak, weight_sum, accumulated = (new_peak, weight_sum, accumulated)
    attn_raw = (accumulated / weight_sum[..., None]).transpose(1, 0, 2)
    attn_normed = rms_scaled(attn_raw, attn_gain)
    combined = (
        (0.5 * (delta_normed + attn_normed))
        .reshape(tokens, local_heads * HEAD_DIM)
        .astype(jnp.bfloat16)
    )
    partial_sum = jnp.dot(combined, out_weight, preferred_element_type=jnp.float32)
    shared = lax.psum_scatter(
        partial_sum.astype(jnp.bfloat16), "head", scatter_dimension=1, tiled=True
    ).astype(jnp.float32)
    return (hidden_in.astype(jnp.float32) + shared).astype(jnp.bfloat16)


def solution(mesh):
    placed = (
        P("seq", "head"),
        P("seq", "head"),
        P("seq", "head"),
        P("seq", "head"),
        P("seq", "head"),
        P("seq", "head"),
        P("seq"),
        P("seq", "head"),
        P("seq", "head"),
        P("seq", "head"),
        P(),
        P(),
        P("head", None),
    )
    return jax.shard_map(
        local, mesh=mesh, in_specs=placed, out_specs=P("seq", "head"), check_vma=False
    )
```

profile of v0, /device:TPU:25, one launch (start us, length us, event | category | flops | bytes accessed | tf_op | source)
XLA Modules:
  0.0 834.3 jit_solution(9774860127785513335)
XLA Ops:
  20.4 59.6 %custom-call.3 = f32[4,3,1,64,64]{3,4,2,1,0:T(8,128)} custom-call(f32[4,3,1,64,64]{4,3,2,1,0:T(8,128)S(1)} %fusion.43), custom_call_target="InvertDiagBlocksLowerTriangular" | custom-call | tf_op jit(solution)/shard_map/triangular_solve | solution.py:102
  83.2 3.3 convolution_bitcast_fusion.4
  86.5 3.3 fusion.34
  91.2 2.3 copy.153
  94.4 10.3 %while.39 = (s32[]{:T(128)}, f32[4,128,128]{1,2,0:T(8,128)S(1)}, f32[4,128,128]{1,2,0:T(8,128)}, f32[3,4,128,128]{2,3,1,0:T(8,128)S(1)}, f32[3,4,128,128]{2,3,1,0:T(8,128)}, /*index=5*/s32[]{:T(128)}, s32[]{:T(128)}) while((s32[]{:T(128)}, f32[4,128,128]{1,2,0:T(8,128)S(1)}, f32[4,128,128]{1,2,0:T(8,128)}, ...), condition=%wide.region_4.5_spmd.clone, body=%wide.region_3.4_spmd.clone.sunk | while | flops 201457664 | bytes 2885218 | solution.py:121
  95.4 2.0 fusion.125
  98.8 2.0 fusion.125
  102.2 2.0 fusion.125
  116.8 2.1 slice_bitcast_fusion.1
  118.9 2.0 fusion.61
  121.0 2.3 fusion.35
  123.3 2.9 iota_compare_fusion
  126.2 131.3 %all-gather.13.cloned.1.call-done = bf16[256,128,128]{2,1,0:T(8,128)(2,1)} async-done(((bf16[4,128,128]{2,1,0:T(8,128)(2,1)}), bf16[256,128,128]{2,1,0:T(8,128)(2,1)}) %all-gather.13.cloned.1.call-update) | async-done | bytes 8388624 | tf_op jit(solution)/shard_map/all_gather | solution.py:17
  257.4 151.0 %all-gather.11.cloned.1.call-done = bf16[256,128,128]{2,1,0:T(8,128)(2,1)} async-done(((bf16[4,128,128]{2,1,0:T(8,128)(2,1)}), bf16[256,128,128]{2,1,0:T(8,128)(2,1)}) %all-gather.11.cloned.1.call-update) | async-done | bytes 8388624 | tf_op jit(solution)/shard_map/all_gather | solution.py:17
  408.4 112.4 %while.37 = (s32[]{:T(128)}, f32[4,128,128]{1,2,0:T(8,128)S(1)}, s32[]{:T(128)}, bf16[64,4,128,128]{3,2,1,0:T(8,128)(2,1)}, bf16[64,4,128,128]{3,2,1,0:T(8,128)(2,1)}, /*index=5*/s32[]{:T(128)}, s32[]{:T(128)}, s32[]{:T(128)}) while((s32[]{:T(128)}, f32[4,128,128]{1,2,0:T(8,128)S(1)}, s32[]{:T(128)}, bf16[64,4,128,128]{3,2,1,0:T(8,128)(2,1)}, ...), condition=%wide.region_6.7_spmd, body=%wide.region_5.6_spmd.sunk | while | flops 100794368 | bytes 1835143 | solution.py:31
  520.9 19.7 %while.38 = (s32[]{:T(128)}, f32[4,128,128]{1,2,0:T(8,128)S(1)}, f32[3,4,64,128]{3,2,1,0:T(8,128)}, f32[3,4,128,128]{2,3,1,0:T(8,128)S(1)}, f32[3,4,128,128]{2,3...) while((s32[]{:T(128)}, f32[4,128,128]{1,2,0:T(8,128)S(1)}, ...), condition=%wide.region_9.10_spmd, body=%wide.region_8.9_spmd.sunk | while | flops 226656256 | bytes 3544197 | solution.py:150
  542.9 46.9 %all-gather.7.cloned.1.call-done = bf16[12288,512]{1,0:T(8,128)(2,1)} async-done(((bf16[192,512]{1,0:T(8,128)(2,1)}), bf16[12288,512]{1,0:T(8,128)(2,1)}) %all-gather.7.cloned.1.call-update) | async-done | bytes 12582928 | tf_op jit(solution)/shard_map/all_gather | solution.py:157
  589.8 16.7 %copy.170 = bf16[12288,512]{0,1:T(8,128)(2,1)} copy(bf16[12288,512]{1,0:T(8,128)(2,1)} %all-gather.7.cloned.1.call-done) | data formatting | bytes 25165824 | tf_op jit(solution)/shard_map/all_gather | solution.py:157
  606.5 19.3 %select_reduce_fusion = (f32[4,192]{1,0:T(4,128)S(1)}, f32[4,192,12288]{2,1,0:T(8,128)}) fusion(pred[192,12288]{1,0:T(8,128)(4,1)} %iota_compare_fusion, bf16[12288,4,128]{0,2,1:T(8,128)(2,1)} %bitcast.202, bf16[192,512]{1,0:T(8,128)(2,1)S(1)} %copy-done.3), kind=kOutput, calls=%fused_computation.40 | convolution fusion | flops 2444229888 | bytes 52890624 | tf_op jit(solution)/shard_map/qhe,khe->hqk/dot_general | solution.py:162
  625.8 17.5 %fusion.29 = f32[4,192]{1,0:T(4,128)S(1)} fusion(f32[4,192,12288]{2,1,0:T(8,128)} %get-tuple-element.288, f32[4,192]{1,0:T(4,128)S(1)} %broadcast_maximum_fusion, pred[192,12288]{1,0:T(8,128)(4,1)} %iota_compare_fusion), kind=kLoop, calls=%fused_computation.41 | loop fusion | flops 37747968 | bytes 40114176 | tf_op jit(solution)/shard_map/reduce_sum | solution.py:170
  643.3 125.6 %all-gather.9.cloned.1.call-done = bf16[12288,512]{1,0:T(8,128)(2,1)} async-done(((bf16[192,512]{1,0:T(8,128)(2,1)}), bf16[12288,512]{1,0:T(8,128)(2,1)}) %all-gather.9.cloned.1.call-update) | async-done | bytes 12582928 | tf_op jit(solution)/shard_map/all_gather | solution.py:158
  768.9 16.7 %copy.173 = bf16[12288,512]{0,1:T(8,128)(2,1)} copy(bf16[12288,512]{1,0:T(8,128)(2,1)} %all-gather.9.cloned.1.call-done) | data formatting | bytes 25165824 | tf_op jit(solution)/shard_map/all_gather | solution.py:158
  785.6 19.2 %multiply_reduce_fusion = (f32[192,4]{0,1:T(4,128)S(1)}, f32[192,4,128]{2,0,1:T(8,128)S(1)}) fusion(f32[192,4]{0,1:T(4,128)S(1)} %bitcast.217, bf16[12288,4,128]{0,2,1:T(8,128)(2,1)} %bitcast.203, f32[4,192,12288]{2,1,0:T(8,128)} %get-tuple-element.288, f32[4,192]{1,0:T(4,128)S(1)} %broadcast_maximum_fusion, pred[192,12288]{1,0:T(8,128)(4,1)} %iota_compare_fusion), kind=kOutput, calls=%fused_computation.78 | convolution fusion | flops 2453961984 | bytes 53093376 | tf_op jit(solution)/shard_map/hqk,khe->hqe/dot_general | solution.py:171
  806.6 19.5 %reduce-scatter.2.cloned.1.call-done = bf16[192,512]{1,0:T(8,128)(2,1)} async-done(((bf16[192,2048]{1,0:T(8,128)(2,1)}), bf16[192,512]{1,0:T(8,128)(2,1)}) %reduce-scatter.2.cloned.1.call-update) | async-done | bytes 196624 | tf_op jit(solution)/shard_map/reduce_scatter | solution.py:186
  (303 shorter events, 171.1 us)
Async XLA Ops:
  6.5 798.6 %copy-start = (bf16[512,2048]{1,0:T(8,128)(2,1)S(1)}, bf16[512,2048]{1,0:T(8,128)(2,1)}, u32[]{:S(2)}) copy-start(bf16[512,2048]{1,0:T(8,128)(2,1)} %param.31) | copy-start | bytes 6291460
  6.5 250.9 %all-gather.13.cloned.1.call-start = ((), (), s32[]{:S(2)}) async-start(), calls=%async_computation.5 | async-start | bytes 8519680 | tf_op jit(solution)/shard_map/all_gather | solution.py:17
  7.1 11.0 %copy-start.6 = (pred[64,64]{1,0:T(8,128)(4,1)}, pred[64,64]{1,0:T(8,128)(4,1)S(1)}, u32[]{:S(2)}) copy-start(pred[64,64]{1,0:T(8,128)(4,1)S(1)} %get-tuple-element.292) | copy-start | bytes 12292
  10.8 3.8 copy-start.7
  11.6 3.0 copy-start.5
  14.7 3.5 copy-start.2
  83.2 3.3 copy-start.1
  106.4 302.0 %all-gather.11.cloned.1.call-start = ((), (), s32[]{:S(2)}) async-start(), calls=%async_computation.4 | async-start | bytes 8519680 | tf_op jit(solution)/shard_map/all_gather | solution.py:17
  107.2 482.5 %all-gather.7.cloned.1.call-start = ((), (), s32[]{:S(2)}) async-start(), calls=%async_computation.1 | async-start | bytes 12779520 | tf_op jit(solution)/shard_map/all_gather | solution.py:157
  108.0 660.9 %all-gather.9.cloned.1.call-start = ((), (), s32[]{:S(2)}) async-start(), calls=%async_computation.2 | async-start | bytes 12779520 | tf_op jit(solution)/shard_map/all_gather | solution.py:158
  108.6 717.6 %reduce-scatter.2.cloned.1.call-start = ((), (), s32[]{:S(2)}) async-start(), calls=%async_computation.3 | async-start | bytes 983040 | tf_op jit(solution)/shard_map/reduce_scatter | solution.py:186
  542.9 63.6 %copy-start.3 = (bf16[192,512]{1,0:T(8,128)(2,1)S(1)}, bf16[192,512]{1,0:T(8,128)(2,1)}, u32[]{:S(2)}) copy-start(bf16[192,512]{1,0:T(8,128)(2,1)} %param.26) | copy-start | bytes 589828
  785.6 19.2 %copy-start.8 = (f32[128]{0:T(128)S(1)}, f32[128]{0:T(128)}, u32[]{:S(2)}) copy-start(f32[128]{0:T(128)} %param.30) | copy-start | bytes 1540
  785.6 19.2 %copy-start.9 = (f32[128]{0:T(128)S(1)}, f32[128]{0:T(128)}, u32[]{:S(2)}) copy-start(f32[128]{0:T(128)} %param.29) | copy-start | bytes 1540
  785.6 40.6 %copy-start.4 = (bf16[192,512]{1,0:T(8,128)(2,1)S(1)}, bf16[192,512]{1,0:T(8,128)(2,1)}, u32[]{:S(2)}) copy-start(bf16[192,512]{1,0:T(8,128)(2,1)} %param.19) | copy-start | bytes 589828
Sparse Core Ops, SparseCore 0:
  106.5 150.8 all-gather.12
  260.9 147.4 all-gather.10
  412.1 177.6 all-gather.6
  593.3 175.5 all-gather.8
  806.7 19.3 reduce-scatter.1
where the time goes:
time: 840 us; the launch traced here: 834 us
  waiting for transfers between devices  475 us (57%)
  matrix products  133 us (16%)
  local copies, waits for them, and re-layouts  113 us (13%)
  other arithmetic  96.1 us (11%)
  between operations  13.4 us (2%)
    all_gather x2, waiting for transfers between devices, prefix(): lax.all_gather(a.astype(kind), axis)  282 us
    all_gather x1, waiting for transfers between devices, local(): lax.all_gather(attn_v, 'seq', axis=0, tiled=True)  126 us
    dot_general x57, matrix products, matmul_heads(): jnp.einsum('hij,hjk->hik', left_side, right_side, precision=HIGHEST_MODE)  70.1 us
    another operation x1, other arithmetic, local(): lax.linalg.triangular_solve(system, right_side, left_side=True, lower=True)  59.6 us
    dynamic_slice x96, local copies, waits for them, and re-layouts, one(): lax.dynamic_index_in_dim(a, hop, 0, False).astype(own.dtype)  50.6 us
    all_gather x1, waiting for transfers between devices, local(): lax.all_gather(attn_k, 'seq', axis=0, tiled=True)  46.9 us
    reduce_scatter x1, waiting for transfers between devices, local(): lax.psum_scatter(partial_sum.astype(jnp.bfloat16), 'head', scatter_dimens...  19.5 us
    dot_general x1, matrix products, local(): jnp.einsum('qhe,khe->hqk', query_heads, key_piece, preferred_element_type...  19.3 us
  transfers between devices with their start and end apart: 5, of which 5 were waited for; matrix products, arithmetic and copies ran while one was open for 24% of the time, Pallas kernels for 0%

commit v1 on v0

v1 whole, which is shorter than its diff:
```python
import jax
import jax.numpy as jnp
from jax import lax
from jax.experimental import pallas as pl
from jax.experimental.pallas import tpu as pltpu
from jax.sharding import PartitionSpec as P

HD = 128
EPSILON = 1e-06
NY, NZ, NX = 4, 8, 2
HEADS = 4
GROUP = 4
SUB = 64
MESH = pl.DeviceIdType.MESH
HIGHEST = lax.Precision.HIGHEST
F32 = jnp.float32
BF16 = jnp.bfloat16
NEG = -1e30
SCALE = HD**-0.5
LOG2E = 1.4426950408889634
Y_ORDER = (0, 1, 3, 2)
UP_HOPS = (4, 4, 3, 3)
DOWN_HOPS = (3, 3, 4, 4)


def mm(a, b):
    return jnp.dot(a.astype(BF16), b.astype(BF16), preferred_element_type=F32)


def mm_nt(a, b, precision=None):
    return lax.dot_general(
        a, b, (((1,), (1,)), ((), ())), precision=precision, preferred_element_type=F32
    )


def mm_tn(a, b):
    return lax.dot_general(
        a.astype(BF16), b.astype(BF16), (((0,), (0,)), ((), ())), preferred_element_type=F32
    )


def place():
    s = lax.axis_index("seq")
    return s // (NZ * NX), (s // NX) % NZ, s % NX


def at(y, z, x):
    return {"seq": ((y % NY) * NZ + z % NZ) * NX + x % NX}


def remote(src, dst, send, recv, device):
    return pltpu.make_async_remote_copy(
        src_ref=src,
        dst_ref=dst,
        send_sem=send,
        recv_sem=recv,
        device_id=device,
        device_id_type=MESH,
    )


def delta_head(h, dq, dk, dv, beta, cum_col, cum_row, low, oloc, qeff, ab_send):
    tokens = dq.shape[0]
    col = slice(h * HD, (h + 1) * HD)
    q = dq[:, col].astype(F32)
    k = dk[:, col].astype(F32)
    v = dv[:, col].astype(F32)
    q = q * (lax.rsqrt(jnp.sum(q * q, axis=-1, keepdims=True) + EPSILON) * SCALE)
    k = k * lax.rsqrt(jnp.sum(k * k, axis=-1, keepdims=True) + EPSILON)
    strength = beta[:, h : h + 1]
    row_id = lax.broadcasted_iota(jnp.int32, (tokens, tokens), 0)
    col_id = lax.broadcasted_iota(jnp.int32, (tokens, tokens), 1)
    c_col, n_col = cum_col[:, h : h + 1], cum_col[:, HEADS : HEADS + 1]
    c_row, n_row = cum_row[h : h + 1, :], cum_row[HEADS : HEADS + 1, :]
    reach = jnp.where(n_col < 0.5, jnp.exp(c_col), 0.0)
    same = (jnp.abs(n_col - n_row) < 0.5) & (row_id >= col_id)
    ratios = jnp.where(same, jnp.exp(jnp.minimum(c_col - c_row, 0.0)), 0.0)
    kb = k.astype(BF16)
    inner = mm_nt(kb, kb)
    system = jnp.where(row_id > col_id, strength * ratios * inner, 0.0)
    near = (row_id // SUB) == (col_id // SUB)
    power = jnp.where(near, -system, 0.0)
    far = jnp.where(near, 0.0, system)
    inverse = jnp.where(row_id == col_id, 1.0, power)
    reached = 2
    while reached < SUB:
        power = mm(power, power)
        inverse = inverse + mm(inverse, power)
        reached *= 2
    right = jnp.concatenate([strength * v, (strength * reach) * k], axis=1)
    solved = mm(inverse, right)
    spread = mm(inverse, far)
    total = solved
    for _ in range((tokens + SUB - 1) // SUB - 1):
        total = solved - mm(spread, total)
    n_last, c_last = n_col[tokens - 1 :, :], c_col[tokens - 1 :, :]
    tail = jnp.where(jnp.abs(n_col - n_last) < 0.5, jnp.exp(jnp.minimum(c_last - c_col, 0.0)), 0.0) * k
    moved = mm_tn(total, tail)
    eye = (row_id == col_id)[:HD, :HD]
    ab_send[h, 0] = (jnp.where(eye, reach[tokens - 1 :, :], 0.0) - moved[HD:]).astype(BF16)
    ab_send[h, 1] = moved[:HD].astype(BF16)
    seen = mm(mm_nt(q.astype(BF16), kb) * ratios, total)
    oloc[:, col] = seen[:, :HD]
    qeff[:, col] = (reach * q - seen[:, HD:]).astype(BF16)


def gather_kernel(
    dq, dk, dv, beta, rows, aq, ak, av,
    kv, qg, sin, oloc, qeff,
    ab_send, ab_recv, t_buf, u_buf, e_buf, s_send,
    own_sem, kv_send, kv_recv, q_send, q_recv, up_send, up_recv, down_send, down_recv,
    c_send, c_recv,
):
    y, z, x = place()
    r, g = (z % 2) * 2 + x, z // 2
    tokens = dq.shape[0]
    across = z + 1 - 2 * (z % 2)
    beyond = z - 1 + 2 * (z % 2)
    peers = [at(y + d, z, x) for d in (1, 2, 3)]
    peers += [at(y + d, z, x + 1) for d in range(4)]
    peers += [at(y, across, x), at(y, across, x + 1), at(y, beyond, x)]
    peers += [at(y, z + d, x) for d in (2, 4, 6)]
    barrier = pltpu.get_barrier_semaphore()
    for peer in peers:
        pl.semaphore_signal(barrier, inc=1, device_id=peer, device_id_type=MESH)
    pl.semaphore_wait(barrier, len(peers))
    sent = []

    def head_cols(h):
        return pl.ds(pl.multiple_of((h % NY) * HD, HD), HD)

    own_k = pltpu.make_async_copy(ak.at[:, head_cols(y)], kv.at[y, z, 0], own_sem.at[0])
    own_v = pltpu.make_async_copy(av.at[:, head_cols(y)], kv.at[y, z, 1], own_sem.at[1])
    own_q = pltpu.make_async_copy(aq.at[:, head_cols(y)], qg.at[y, x], own_sem.at[2])
    own_k.start()
    own_v.start()
    for j in (1, 2, 3):
        to = y - Y_ORDER[j] + NY
        for part, source in enumerate((ak, av)):
            copy = remote(
                source.at[:, head_cols(to)], kv.at[y, z, part],
                kv_send.at[j, part], kv_recv.at[j, part], at(to, z, x),
            )
            copy.start()
            sent.append(copy)

    def piece(j, zz):
        return kv.at[(y + Y_ORDER[j]) % NY, zz % NZ]

    def up(j, hop):
        block = piece(j, z - hop + NZ)
        copy = remote(block, block, up_send.at[j, hop], up_recv.at[j, hop], at(y, z + 1, x))
        copy.start()
        sent.append(copy)

    def down(j, hop):
        block = piece(j, z + hop)
        copy = remote(block, block, down_send.at[j, hop], down_recv.at[j, hop], at(y, z - 1 + NZ, x))
        copy.start()
        sent.append(copy)

    def up_arrived(j, hop):
        block = piece(j, z - hop + NZ)
        remote(block, block, up_send.at[j, hop - 1], up_recv.at[j, hop - 1], at(y, z + 1, x)).wait_recv()

    def down_arrived(j, hop):
        block = piece(j, z + hop)
        remote(block, block, down_send.at[j, hop - 1], down_recv.at[j, hop - 1], at(y, z + 1, x)).wait_recv()

    own_k.wait()
    own_v.wait()
    up(0, 0)
    down(0, 0)
    own_q.start()
    for d in range(4):
        for dx in range(2):
            if d or dx:
                to = y + d
                copy = remote(
                    aq.at[:, head_cols(to)], qg.at[y, x],
                    q_send.at[d, dx], q_recv.at[(NY - d) % NY, dx], at(to, z, x + dx),
                )
                copy.start()
                sent.append(copy)

    low = (
        lax.broadcasted_iota(jnp.int32, (tokens, tokens), 0)
        >= lax.broadcasted_iota(jnp.int32, (tokens, tokens), 1)
    ).astype(F32)
    cum_col = mm_nt(low, rows[...], HIGHEST)
    cum_row = mm_nt(rows[...], low, HIGHEST)

    def first_round(j):
        for part in range(2):
            block = kv.at[(y + Y_ORDER[j]) % NY, z, part]
            remote(block, block, kv_send.at[j, part], kv_recv.at[j, part], at(y + 1, z, x)).wait_recv()
        up(j, 0)
        down(j, 0)

    def later_round(j, hop):
        if hop <= UP_HOPS[j]:
            up_arrived(j, hop)
            if hop < UP_HOPS[j]:
                up(j, hop)
        if hop <= DOWN_HOPS[j]:
            down_arrived(j, hop)
            if hop < DOWN_HOPS[j]:
                down(j, hop)

    for h in range(HEADS):
        delta_head(h, dq, dk, dv, beta, cum_col, cum_row, low, oloc, qeff, ab_send)
        if h:
            first_round(h)

    def of_group(index):
        return at(y, g * 2 + (index % GROUP) // 2, (index % GROUP) % 2)

    def pairs_out():
        for d in (1, 2, 3):
            to = (r + d) % GROUP
            copy = remote(ab_send.at[to], ab_recv.at[r], c_send.at[0, d], c_recv.at[0, d], of_group(to))
            copy.start()
            sent.append(copy)
        ab_recv[r] = ab_send[r]

    def pairs_in():
        for d in (1, 2, 3):
            block = ab_recv.at[(r - d + GROUP) % GROUP]
            remote(block, block, c_send.at[0, d], c_recv.at[0, d], of_group(r + 1)).wait_recv()

    def exchange_out(level, buf, mine, device):
        for d in (1, 2, 3):
            copy = remote(buf.at[mine], buf.at[mine], c_send.at[level, d], c_recv.at[level, d], device(d))
            copy.start()
            sent.append(copy)

    def exchange_in(level, buf, mine, device):
        for d in (1, 2, 3):
            block = buf.at[(mine - d + GROUP) % GROUP]
            remote(block, block, c_send.at[level, d], c_recv.at[level, d], device(d)).wait_recv()

    def fold(buf):
        before = []
        a, b = buf[0, 0].astype(F32), buf[0, 1].astype(F32)
        for i in range(1, GROUP):
            before.append((a, b))
            both = mm(jnp.concatenate([a, b], axis=0), buf[i, 0])
            a, b = both[:HD], both[HD:] + buf[i, 1].astype(F32)
        return before, (a, b)

    in_chain = lambda d: at(y, z + 2 * d, x)
    in_column = lambda d: at(y + d, z, x)

    def level_one():
        pairs_in()
        before, (a, b) = fold(ab_recv)
        for i, (ea, eb) in enumerate(before):
            e_buf[i, 0] = ea
            e_buf[i, 1] = eb
        t_buf[g, 0] = a.astype(BF16)
        t_buf[g, 1] = b.astype(BF16)
        exchange_out(1, t_buf, g, in_chain)

    def level_two():
        exchange_in(1, t_buf, g, in_chain)
        before, (a, b) = fold(t_buf)
        eye = (
            lax.broadcasted_iota(jnp.int32, (HD, HD), 0) == lax.broadcasted_iota(jnp.int32, (HD, HD), 1)
        ).astype(F32)
        fa, fb = eye, jnp.zeros((HD, HD), F32)
        for i, (ea, eb) in enumerate(before):
            fa = jnp.where(g == i + 1, ea, fa)
            fb = jnp.where(g == i + 1, eb, fb)
        e_buf[3, 0] = fa
        e_buf[3, 1] = fb
        u_buf[y, 0] = a.astype(BF16)
        u_buf[y, 1] = b.astype(BF16)
        exchange_out(2, u_buf, y, in_column)

    def level_three():
        exchange_in(2, u_buf, y, in_column)
        state = jnp.zeros((HD, HD), F32)
        b = u_buf[0, 1].astype(F32)
        for i in range(1, NY):
            state = jnp.where(y == i, b, state)
            if i < NY - 1:
                b = mm(b, u_buf[i, 0]) + u_buf[i, 1].astype(F32)
        state = mm(state, e_buf[3, 0]) + e_buf[3, 1]
        s_send[0] = state.astype(BF16)
        for i in range(3):
            s_send[i + 1] = (mm(state, e_buf[i, 0]) + e_buf[i, 1]).astype(BF16)
        for d in (1, 2, 3):
            to = (r + d) % GROUP
            copy = remote(s_send.at[to], sin.at[r], c_send.at[3, d], c_recv.at[3, d], of_group(to))
            copy.start()
            sent.append(copy)
        sin[r] = s_send[r]

    def states_in():
        for d in (1, 2, 3):
            block = sin.at[(r - d + GROUP) % GROUP]
            remote(block, block, c_send.at[3, d], c_recv.at[3, d], of_group(r + 1)).wait_recv()

    pairs_out()
    steps = [(j, hop) for hop in (1, 2, 3, 4) for j in range(4)]
    stages = {2: level_one, 5: level_two, 8: level_three}
    for n, (j, hop) in enumerate(steps):
        if n in stages:
            stages[n]()
        later_round(j, hop)
    states_in()
    own_q.wait()
    for d in range(4):
        for dx in range(2):
            if d or dx:
                block = qg.at[(y + d) % NY, (x + dx) % NX]
                remote(block, block, q_send.at[d, dx], q_recv.at[d, dx], at(y + d, z, x + dx)).wait_recv()
    for copy in sent:
        copy.wait_send()


def attend_kernel(kv, q, o, lse, m_ref, l_ref, acc_ref):
    y, z, x = place()
    tokens = kv.shape[3]
    wide = 2 * tokens
    keys = 2 * tokens
    factor = SCALE * LOG2E

    def block(yy, zp, queries, masked):
        k = jnp.concatenate([kv[yy, 2 * zp, 0], kv[yy, 2 * zp + 1, 0]], axis=0)
        v = jnp.concatenate([kv[yy, 2 * zp, 1], kv[yy, 2 * zp + 1, 1]], axis=0)
        s = mm_nt(k, queries)
        if masked:
            row = lax.broadcasted_iota(jnp.int32, (keys, wide), 0)
            col = lax.broadcasted_iota(jnp.int32, (keys, wide), 1)
            key_at = zp * (4 * tokens) + x * tokens + row + jnp.where(row >= tokens, tokens, 0)
            seen = key_at <= z * wide + col
            s = jnp.where(seen, s, NEG)
        old = m_ref[...]
        new = jnp.maximum(old, jnp.max(s, axis=0, keepdims=True))
        p = jnp.exp2((s - new) * factor)
        if masked:
            p = jnp.where(seen, p, 0.0)
        shrink = jnp.exp2((old - new) * factor)
        l_ref[...] = l_ref[...] * shrink + jnp.sum(p, axis=0, keepdims=True)
        acc_ref[...] = acc_ref[...] * shrink + mm_tn(v, p)
        m_ref[...] = new

    for yq in range(NY):
        queries = jnp.concatenate([q[yq, 0], q[yq, 1]], axis=0)
        m_ref[...] = jnp.full_like(m_ref, NEG)
        l_ref[...] = jnp.zeros_like(l_ref)
        acc_ref[...] = jnp.zeros_like(acc_ref)

        @pl.loop(0, yq * (NZ // 2))
        def _(n):
            block(n // (NZ // 2), n % (NZ // 2), queries, False)

        @pl.loop(0, z // 2)
        def _(n):
            block(yq, n, queries, False)

        block(yq, z // 2, queries, True)
        total = l_ref[...]
        some = total > 0.0
        safe = jnp.where(some, total, 1.0)
        out = acc_ref[...] / safe
        o[yq] = out.T.astype(BF16)
        level = jnp.where(some, m_ref[...] * factor + jnp.log2(safe), NEG)
        lse[yq] = jnp.broadcast_to(level, (8, wide))


def finish_kernel(
    o, lse, hidden, weight, oloc, qeff, sin, dgain, again,
    out,
    o_recv, lse_recv, part, part_recv,
    o_send_sem, o_recv_sem, l_send_sem, l_recv_sem, w_send_sem, w_recv_sem,
):
    y, z, x = place()
    me = lax.axis_index("head")
    tokens, cols = hidden.shape
    others = [(d, dx) for d in range(4) for dx in range(2) if d or dx]
    barrier = pltpu.get_barrier_semaphore()
    for d, dx in others:
        pl.semaphore_signal(barrier, inc=1, device_id=at(y + d, z, x + dx), device_id_type=MESH)
    for d in (1, 2, 3):
        pl.semaphore_signal(barrier, inc=1, device_id={"head": (me + d) % 4}, device_id_type=MESH)
    pl.semaphore_wait(barrier, len(others) + 3)
    sent = []
    for d, dx in others:
        ty, tx = (y + d) % NY, (x + dx) % NX
        rows = pl.ds(pl.multiple_of(tx * tokens, 64), tokens)
        copy = remote(
            o.at[ty, rows], o_recv.at[y, x],
            o_send_sem.at[d, dx], o_recv_sem.at[(NY - d) % NY, dx], at(ty, z, tx),
        )
        copy.start()
        sent.append(copy)
        copy = remote(
            lse.at[ty], lse_recv.at[y, x],
            l_send_sem.at[d, dx], l_recv_sem.at[(NY - d) % NY, dx], at(ty, z, tx),
        )
        copy.start()
        sent.append(copy)
    o_recv[y, x] = o[y, pl.ds(pl.multiple_of(x * tokens, 64), tokens), :]
    lse_recv[y, x] = lse[y]

    delta = []
    for h in range(HEADS):
        col = slice(h * HD, (h + 1) * HD)
        raw = mm_nt(qeff[:, col], sin[h]) + oloc[:, col]
        scaled = raw * lax.rsqrt(jnp.mean(raw * raw, axis=-1, keepdims=True) + EPSILON)
        delta.append(scaled * dgain[...])

    for d, dx in others:
        block = o_recv.at[(y + d) % NY, (x + dx) % NX]
        remote(block, block, o_send_sem.at[d, dx], o_recv_sem.at[d, dx], at(y + d, z, x + dx)).wait_recv()
        block = lse_recv.at[(y + d) % NY, (x + dx) % NX]
        remote(block, block, l_send_sem.at[d, dx], l_recv_sem.at[d, dx], at(y + d, z, x + dx)).wait_recv()

    shares = []
    for h in range(HEADS):
        a, b = lse_recv[h, 0][:1], lse_recv[h, 1][:1]
        top = jnp.maximum(a, b)
        a, b = jnp.exp2(a - top), jnp.exp2(b - top)
        both = a + b
        shares += [a / both, b / both]
    shares = jnp.concatenate(shares, axis=0)
    pick = (
        lax.broadcasted_iota(jnp.int32, (tokens, 2 * tokens), 1)
        == lax.broadcasted_iota(jnp.int32, (tokens, 2 * tokens), 0) + x * tokens
    ).astype(F32)
    shares = mm_nt(pick, shares, HIGHEST)
    combined = []
    for h in range(HEADS):
        raw = (
            o_recv[h, 0].astype(F32) * shares[:, 2 * h : 2 * h + 1]
            + o_recv[h, 1].astype(F32) * shares[:, 2 * h + 1 : 2 * h + 2]
        )
        scaled = raw * lax.rsqrt(jnp.mean(raw * raw, axis=-1, keepdims=True) + EPSILON)
        combined.append((0.5 * (delta[h] + scaled * again[...])).astype(BF16))
    combined = jnp.concatenate(combined, axis=1)
    for d in (1, 2, 3):
        to = (me + d) % 4
        columns = pl.ds(pl.multiple_of(to * cols, HD), cols)
        part[d] = jnp.dot(combined, weight[:, columns], preferred_element_type=F32).astype(BF16)
        copy = remote(part.at[d], part_recv.at[d], w_send_sem.at[d], w_recv_sem.at[d], {"head": to})
        copy.start()
        sent.append(copy)
    total = jnp.dot(
        combined, weight[:, pl.ds(pl.multiple_of(me * cols, HD), cols)], preferred_element_type=F32
    )
    for d in (1, 2, 3):
        block = part_recv.at[d]
        remote(block, block, w_send_sem.at[d], w_recv_sem.at[d], {"head": (me + d) % 4}).wait_recv()
        total = total + part_recv[d].astype(F32)
    out[...] = (hidden[...].astype(F32) + total).astype(BF16)
    for copy in sent:
        copy.wait_send()


VMEM = pl.BlockSpec(memory_space=pltpu.VMEM)
ANY = pl.BlockSpec(memory_space=pl.ANY)
DMA = pltpu.SemaphoreType.DMA
LIMIT = 48 * 1024 * 1024


def local(
    hidden_in, delta_q, delta_k, delta_v, beta, log_decay, resets,
    attn_q, attn_k, attn_v, delta_gain, attn_gain, out_weight,
):
    tokens, cols = delta_q.shape
    struct = jax.ShapeDtypeStruct
    rows = jnp.concatenate(
        [log_decay.T, resets.astype(F32)[None], jnp.zeros((3, tokens), F32)], axis=0
    )
    kv, qg, sin, oloc, qeff = pl.pallas_call(
        gather_kernel,
        out_shape=(
            struct((NY, NZ, 2, tokens, HD), BF16),
            struct((NY, NX, tokens, HD), BF16),
            struct((HEADS, HD, HD), BF16),
            struct((tokens, cols), F32),
            struct((tokens, cols), BF16),
        ),
        in_specs=[VMEM] * 8,
        out_specs=(ANY, ANY, VMEM, VMEM, VMEM),
        scratch_shapes=[
            pltpu.VMEM((HEADS, 2, HD, HD), BF16),
            pltpu.VMEM((GROUP, 2, HD, HD), BF16),
            pltpu.VMEM((GROUP, 2, HD, HD), BF16),
            pltpu.VMEM((NY, 2, HD, HD), BF16),
            pltpu.VMEM((4, 2, HD, HD), F32),
            pltpu.VMEM((GROUP, HD, HD), BF16),
            DMA((3,)),
            DMA((4, 2)), DMA((4, 2)),
            DMA((4, 2)), DMA((4, 2)),
            DMA((4, 4)), DMA((4, 4)),
            DMA((4, 4)), DMA((4, 4)),
            DMA((4, 4)), DMA((4, 4)),
        ],
        compiler_params=pltpu.CompilerParams(
            collective_id=0, has_side_effects=True, vmem_limit_bytes=LIMIT
        ),
    )(delta_q, delta_k, delta_v, beta, rows, attn_q, attn_k, attn_v)
    o, lse = pl.pallas_call(
        attend_kernel,
        out_shape=(struct((NY, NX * tokens, HD), BF16), struct((NY, 8, NX * tokens), F32)),
        in_specs=[VMEM] * 2,
        out_specs=(VMEM, VMEM),
        scratch_shapes=[
            pltpu.VMEM((1, NX * tokens), F32),
            pltpu.VMEM((1, NX * tokens), F32),
            pltpu.VMEM((HD, NX * tokens), F32),
        ],
        compiler_params=pltpu.CompilerParams(vmem_limit_bytes=LIMIT),
    )(kv, qg)
    return pl.pallas_call(
        finish_kernel,
        out_shape=struct((tokens, cols), BF16),
        in_specs=[VMEM] * 9,
        out_specs=VMEM,
        scratch_shapes=[
            pltpu.VMEM((NY, NX, tokens, HD), BF16),
            pltpu.VMEM((NY, NX, 8, NX * tokens), F32),
            pltpu.VMEM((4, tokens, cols), BF16),
            pltpu.VMEM((4, tokens, cols), BF16),
            DMA((4, 2)), DMA((4, 2)),
            DMA((4, 2)), DMA((4, 2)),
            DMA((4,)), DMA((4,)),
        ],
        compiler_params=pltpu.CompilerParams(
            collective_id=1, has_side_effects=True, vmem_limit_bytes=LIMIT
        ),
    )(
        o, lse, hidden_in, out_weight, oloc, qeff, sin,
        delta_gain.reshape(1, HD), attn_gain.reshape(1, HD),
    )


def solution(mesh):
    by_head = P("seq", "head")
    placed = (by_head,) * 6 + (P("seq"),) + (by_head,) * 3 + (P(), P(), P("head", None))
    return jax.shard_map(local, mesh=mesh, in_specs=placed, out_specs=by_head, check_vma=False)
```

time: 840 us -> 106 us (0.13)
  the two profiles are of different devices: /device:TPU:25 before, /device:TPU:227 now
where the time goes in v1:
time: 106 us
  Pallas kernels  97.2 us (92%)
  local copies, waits for them, and re-layouts  7.12 us (7%)
  other arithmetic  1.57 us (1%)
    pallas_call x1, Pallas kernels, local(): pl.pallas_call(gather_kernel, out_shape=(struct((NY, NZ, 2, tokens, HD),...  48.3 us
    pallas_call x1, Pallas kernels, local(): pl.pallas_call(finish_kernel, out_shape=struct((tokens, cols), BF16), in_...  24.7 us
    pallas_call x1, Pallas kernels, local(): pl.pallas_call(attend_kernel, out_shape=(struct((NY, NX * tokens, HD), BF...  24.2 us
    unnamed x22, local copies, waits for them, and re-layouts  7.05 us

profile of v1, /device:TPU:227, one launch (start us, length us, event | category | flops | bytes accessed | tf_op | source)
XLA Modules:
  0.0 105.9 jit_solution(1375193513711261391)
XLA Ops:
  0.0 0.0 copy-start
  0.0 0.1 pad.2.clone
  0.1 0.8 convert_element_type.3
  0.9 0.8 maximum_maximum_fusion.rows
  1.7 0.8 copy.14.beta
  2.5 0.0 copy-start.1
  2.5 0.9 copy-done.1
  3.4 0.0 copy-start.2
  3.4 0.9 copy-done.2
  4.3 0.0 copy-start.3
  4.3 0.9 copy-done.3
  5.2 0.0 copy-start.4
  5.2 0.9 copy-done.4
  6.2 0.0 copy-start.5
  6.2 0.9 copy-done.5
  7.1 0.9 copy-done.6
  8.0 48.3 %shard_map.127 = (bf16[4,8,2,192,128]{4,3,2,1,0:T(8,128)(2,1)S(1)}, bf16[4,2,192,128]{3,2,1,0:T(8,128)(2,1)S(1)}, bf16[4,128,128]{2,1,0:T(8,128)(2,1)S(1)}, f32[192,512]{1,0:T(8,128)S(1)}, bf16[192,512]{1,0:T(8,128)(2,1)S(1)}) custom-call(bf16[192,512]{1,0:T(8,128)(2,1)S(1)} %copy-done.1, bf16[192,512]{1,0:T(8,128)(2,1)S(1)} %copy-done.2, ...), custom_call_target="tpu_custom_call" | custom-call | tf_op jit(solution)/shard_map/pallas_call | solution.py:477
  56.4 24.2 %shard_map.128 = (bf16[4,384,128]{2,1,0:T(8,128)(2,1)S(1)}, f32[4,8,384]{2,1,0:T(8,128)S(1)}) custom-call(bf16[4,8,2,192,128]{4,3,2,1,0:T(8,128)(2,1)S(1)} %get-tuple-element.12.kv, bf16[4,2,192,128]{3,2,1,0:T(8,128)(2,1)S(1)} %get-tuple-element.13.q), custom_call_target="tpu_custom_call" | custom-call | tf_op jit(solution)/shard_map/pallas_call | solution.py:506
  80.5 0.0 copy-done
  80.5 0.0 copy-done.7
  80.5 0.0 copy-done.8
  80.5 0.0 copy-done.9
  80.6 24.7 %shard_map.129 = bf16[192,512]{1,0:T(8,128)(2,1)S(1)} custom-call(bf16[4,384,128]{2,1,0:T(8,128)(2,1)S(1)} %get-tuple-element.14.o, f32[4,8,384]{2,1,0:T(8,128)S(1)} %get-tuple-element.15.lse, bf16[192,512]{1,0:T(8,128)(2,1)S(1)} %copy-done.7, bf16[512,2048]{1,0:T(8,128)(2,1)S(1)} %copy-done, f32[192,512]{1,0:T(8,128)S(1)} %get-tuple-element.16.oloc, ...), custom_call_target="tpu_custom_call" | custom-call | tf_op jit(solution)/shard_map/pallas_call | solution.py:518
  105.3 0.7 copy.16
  (5 shorter events, 0.0 us)
Async XLA Ops:
  0.0 80.5 %copy-start = (bf16[512,2048]{1,0:T(8,128)(2,1)S(1)}, bf16[512,2048]{1,0:T(8,128)(2,1)}, u32[]{:S(2)}) copy-start(bf16[512,2048]{1,0:T(8,128)(2,1)} %weight.1) | copy-start | bytes 6291460
  2.5 0.9 copy-start.1
  3.4 0.9 copy-start.2
  4.3 0.9 copy-start.3
  5.2 0.9 copy-start.4
  6.2 0.9 copy-start.5
  7.1 0.9 copy-start.6
  8.0 72.5 %copy-start.7 = (bf16[192,512]{1,0:T(8,128)(2,1)S(1)}, bf16[192,512]{1,0:T(8,128)(2,1)}, u32[]{:S(2)}) copy-start(bf16[192,512]{1,0:T(8,128)(2,1)} %hidden.1) | copy-start | bytes 589828
  8.0 72.5 %copy-start.8 = (f32[128]{0:T(128)S(1)}, f32[128]{0:T(128)}, u32[]{:S(2)}) copy-start(f32[128]{0:T(128)} %param.23) | copy-start | bytes 1540
  8.0 72.5 %copy-start.9 = (f32[128]{0:T(128)S(1)}, f32[128]{0:T(128)}, u32[]{:S(2)}) copy-start(f32[128]{0:T(128)} %param.24) | copy-start | bytes 1540

commit v2 on v1

--- a/solution.py
+++ b/solution.py
@@ -59,7 +59,7 @@
     )
 
 
-def delta_head(h, dq, dk, dv, beta, cum_col, cum_row, low, oloc, qeff, ab_send):
+def delta_head(h, dq, dk, dv, betas, cum_col, cum_row, oloc, qeff, ab_send):
     tokens = dq.shape[0]
     col = slice(h * HD, (h + 1) * HD)
     q = dq[:, col].astype(F32)
@@ -67,7 +67,7 @@
     v = dv[:, col].astype(F32)
     q = q * (lax.rsqrt(jnp.sum(q * q, axis=-1, keepdims=True) + EPSILON) * SCALE)
     k = k * lax.rsqrt(jnp.sum(k * k, axis=-1, keepdims=True) + EPSILON)
-    strength = beta[:, h : h + 1]
+    strength = betas[:, h + 8 : h + 9]
     row_id = lax.broadcasted_iota(jnp.int32, (tokens, tokens), 0)
     col_id = lax.broadcasted_iota(jnp.int32, (tokens, tokens), 1)
     c_col, n_col = cum_col[:, h : h + 1], cum_col[:, HEADS : HEADS + 1]
@@ -104,16 +104,44 @@
     qeff[:, col] = (reach * q - seen[:, HD:]).astype(BF16)
 
 
-def gather_kernel(
-    dq, dk, dv, beta, rows, aq, ak, av,
-    kv, qg, sin, oloc, qeff,
+def attend(tiles, k, v, q, m_ref, l_ref, acc_ref, seen=None):
+    factor = SCALE * LOG2E
+    scores = [mm_nt(k, q[t]) for t in tiles]
+    for t, s in zip(tiles, scores):
+        if seen is not None:
+            s = jnp.where(seen, s, NEG)
+        old = m_ref[t]
+        new = jnp.maximum(old, jnp.max(s, axis=0, keepdims=True))
+        p = jnp.exp2((s - new) * factor)
+        if seen is not None:
+            p = jnp.where(seen, p, 0.0)
+        shrink = jnp.exp2((old - new) * factor)
+        l_ref[t] = l_ref[t] * shrink + jnp.sum(p, axis=0, keepdims=True)
+        acc_ref[t] = acc_ref[t] * shrink + mm_tn(v, p)
+        m_ref[t] = new
+
+
+def main_kernel(
+    dq_in, dk_in, dv_in, beta_in, decay_in, resets_in, aq, ak, av,
+    o, lse, sin, oloc, qeff,
+    dq, dk, dv, beta, decay, resets, rows,
+    kv, qg, m_ref, l_ref, acc_ref,
     ab_send, ab_recv, t_buf, u_buf, e_buf, s_send,
-    own_sem, kv_send, kv_recv, q_send, q_recv, up_send, up_recv, down_send, down_recv,
+    in_sem, own_sem, kv_send, kv_recv, q_send, q_recv, up_send, up_recv, down_send, down_recv,
     c_send, c_recv,
 ):
     y, z, x = place()
     r, g = (z % 2) * 2 + x, z // 2
     tokens = dq.shape[0]
+    wide = NX * tokens
+    loads = [
+        pltpu.make_async_copy(a, b, in_sem.at[i])
+        for i, (a, b) in enumerate(
+            zip((dq_in, dk_in, dv_in, beta_in, decay_in, resets_in), (dq, dk, dv, beta, decay, resets))
+        )
+    ]
+    for load in loads:
+        load.start()
     across = z + 1 - 2 * (z % 2)
     beyond = z - 1 + 2 * (z % 2)
     peers = [at(y + d, z, x) for d in (1, 2, 3)]
@@ -129,9 +157,12 @@
     def head_cols(h):
         return pl.ds(pl.multiple_of((h % NY) * HD, HD), HD)
 
+    def q_rows(xx):
+        return pl.ds(pl.multiple_of((xx % NX) * tokens, 64), tokens)
+
     own_k = pltpu.make_async_copy(ak.at[:, head_cols(y)], kv.at[y, z, 0], own_sem.at[0])
     own_v = pltpu.make_async_copy(av.at[:, head_cols(y)], kv.at[y, z, 1], own_sem.at[1])
-    own_q = pltpu.make_async_copy(aq.at[:, head_cols(y)], qg.at[y, x], own_sem.at[2])
+    own_q = pltpu.make_async_copy(aq.at[:, head_cols(y)], qg.at[y, q_rows(x)], own_sem.at[2])
     own_k.start()
     own_v.start()
     for j in (1, 2, 3):
@@ -144,73 +175,74 @@
             copy.start()
             sent.append(copy)
 
-    def piece(j, zz):
-        return kv.at[(y + Y_ORDER[j]) % NY, zz % NZ]
-
-    def up(j, hop):
-        block = piece(j, z - hop + NZ)
-        copy = remote(block, block, up_send.at[j, hop], up_recv.at[j, hop], at(y, z + 1, x))
-        copy.start()
-        sent.append(copy)
-
-    def down(j, hop):
-        block = piece(j, z + hop)
-        copy = remote(block, block, down_send.at[j, hop], down_recv.at[j, hop], at(y, z - 1 + NZ, x))
-        copy.start()
-        sent.append(copy)
-
-    def up_arrived(j, hop):
-        block = piece(j, z - hop + NZ)
+    def y_of(j):
+        step = Y_ORDER[j] if isinstance(j, int) else j + jnp.where(j == 2, 1, 0) - jnp.where(j == 3, 1, 0)
+        return (y + step) % NY
+
+    def upward(j, hop):
+        block = kv.at[y_of(j), (z - hop + NZ) % NZ]
+        return remote(block, block, up_send.at[j, hop], up_recv.at[j, hop], at(y, z + 1, x))
+
+    def downward(j, hop):
+        block = kv.at[y_of(j), (z + hop) % NZ]
+        return remote(block, block, down_send.at[j, hop], down_recv.at[j, hop], at(y, z - 1 + NZ, x))
+
+    def arrive_up(j, hop):
+        block = kv.at[y_of(j), (z - hop + NZ) % NZ]
         remote(block, block, up_send.at[j, hop - 1], up_recv.at[j, hop - 1], at(y, z + 1, x)).wait_recv()
 
-    def down_arrived(j, hop):
-        block = piece(j, z + hop)
+    def arrive_down(j, hop):
+        block = kv.at[y_of(j), (z + hop) % NZ]
         remote(block, block, down_send.at[j, hop - 1], down_recv.at[j, hop - 1], at(y, z + 1, x)).wait_recv()
 
     own_k.wait()
     own_v.wait()
-    up(0, 0)
-    down(0, 0)
+    upward(0, 0).start()
+    downward(0, 0).start()
     own_q.start()
     for d in range(4):
         for dx in range(2):
             if d or dx:
                 to = y + d
                 copy = remote(
-                    aq.at[:, head_cols(to)], qg.at[y, x],
+                    aq.at[:, head_cols(to)], qg.at[y, q_rows(x)],
                     q_send.at[d, dx], q_recv.at[(NY - d) % NY, dx], at(to, z, x + dx),
                 )
                 copy.start()
                 sent.append(copy)
 
-    low = (
-        lax.broadcasted_iota(jnp.int32, (tokens, tokens), 0)
-        >= lax.broadcasted_iota(jnp.int32, (tokens, tokens), 1)
-    ).astype(F32)
+    for load in loads:
+        load.wait()
+    rows[...] = jnp.zeros_like(rows)
+    rows[0:HEADS] = decay[...]
+    rows[HEADS : HEADS + 1] = resets[...].astype(F32)
+    rows[8 : 8 + HEADS] = beta[...]
+    row_id = lax.broadcasted_iota(jnp.int32, (tokens, tokens), 0)
+    col_id = lax.broadcasted_iota(jnp.int32, (tokens, tokens), 1)
+    low = (row_id >= col_id).astype(F32)
     cum_col = mm_nt(low, rows[...], HIGHEST)
     cum_row = mm_nt(rows[...], low, HIGHEST)
+    betas = mm_nt((row_id == col_id).astype(F32), rows[...], HIGHEST)
 
     def first_round(j):
         for part in range(2):
-            block = kv.at[(y + Y_ORDER[j]) % NY, z, part]
+            block = kv.at[y_of(j), z, part]
             remote(block, block, kv_send.at[j, part], kv_recv.at[j, part], at(y + 1, z, x)).wait_recv()
-        up(j, 0)
-        down(j, 0)
-
-    def later_round(j, hop):
-        if hop <= UP_HOPS[j]:
-            up_arrived(j, hop)
-            if hop < UP_HOPS[j]:
-                up(j, hop)
-        if hop <= DOWN_HOPS[j]:
-            down_arrived(j, hop)
-            if hop < DOWN_HOPS[j]:
-                down(j, hop)
+        upward(j, 0).start()
+        downward(j, 0).start()
+
+    def forward_both(j, hop):
+        arrive_up(j, hop)
+        upward(j, hop).start()
+        arrive_down(j, hop)
+        downward(j, hop).start()
 
     for h in range(HEADS):
-        delta_head(h, dq, dk, dv, beta, cum_col, cum_row, low, oloc, qeff, ab_send)
+        delta_head(h, dq, dk, dv, betas, cum_col, cum_row, oloc, qeff, ab_send)
         if h:
             first_round(h)
+        if h >= 2:
+            forward_both(h - 2, 1)
 
     def of_group(index):
         return at(y, g * 2 + (index % GROUP) // 2, (index % GROUP) % 2)
@@ -228,11 +260,11 @@
             block = ab_recv.at[(r - d + GROUP) % GROUP]
             remote(block, block, c_send.at[0, d], c_recv.at[0, d], of_group(r + 1)).wait_recv()
 
-    def exchange_out(level, buf, mine, device):
-        for d in (1, 2, 3):
-            copy = remote(buf.at[mine], buf.at[mine], c_send.at[level, d], c_recv.at[level, d], device(d))
-            copy.start()
-            sent.append(copy)
+    def exchange(level, buf, mine, device):
+        return [
+            remote(buf.at[mine], buf.at[mine], c_send.at[level, d], c_recv.at[level, d], device(d))
+            for d in (1, 2, 3)
+        ]
 
     def exchange_in(level, buf, mine, device):
         for d in (1, 2, 3):
@@ -259,14 +291,13 @@
             e_buf[i, 1] = eb
         t_buf[g, 0] = a.astype(BF16)
         t_buf[g, 1] = b.astype(BF16)
-        exchange_out(1, t_buf, g, in_chain)
+        for copy in exchange(1, t_buf, g, in_chain):
+            copy.start()
 
     def level_two():
         exchange_in(1, t_buf, g, in_chain)
         before, (a, b) = fold(t_buf)
-        eye = (
-            lax.broadcasted_iota(jnp.int32, (HD, HD), 0) == lax.broadcasted_iota(jnp.int32, (HD, HD), 1)
-        ).astype(F32)
+        eye = (row_id == col_id)[:HD, :HD].astype(F32)
         fa, fb = eye, jnp.zeros((HD, HD), F32)
         for i, (ea, eb) in enumerate(before):
             fa = jnp.where(g == i + 1, ea, fa)
@@ -275,7 +306,15 @@
         e_buf[3, 1] = fb
         u_buf[y, 0] = a.astype(BF16)
         u_buf[y, 1] = b.astype(BF16)
-        exchange_out(2, u_buf, y, in_column)
+        for copy in exchange(2, u_buf, y, in_column):
+            copy.start()
+
+    def states_out():
+        copies = []
+        for d in (1, 2, 3):
+            to = (r + d) % GROUP
+            copies.append(remote(s_send.at[to], sin.at[r], c_send.at[3, d], c_recv.at[3, d], of_group(to)))
+        return copies
 
     def level_three():
         exchange_in(2, u_buf, y, in_column)
@@ -289,11 +328,8 @@
         s_send[0] = state.astype(BF16)
         for i in range(3):
             s_send[i + 1] = (mm(state, e_buf[i, 0]) + e_buf[i, 1]).astype(BF16)
-        for d in (1, 2, 3):
-            to = (r + d) % GROUP
-            copy = remote(s_send.at[to], sin.at[r], c_send.at[3, d], c_recv.at[3, d], of_group(to))
+        for copy in states_out():
             copy.start()
-            sent.append(copy)
         sin[r] = s_send[r]
 
     def states_in():
@@ -302,72 +338,97 @@
             remote(block, block, c_send.at[3, d], c_recv.at[3, d], of_group(r + 1)).wait_recv()
 
     pairs_out()
-    steps = [(j, hop) for hop in (1, 2, 3, 4) for j in range(4)]
-    stages = {2: level_one, 5: level_two, 8: level_three}
-    for n, (j, hop) in enumerate(steps):
-        if n in stages:
-            stages[n]()
-        later_round(j, hop)
-    states_in()
+    forward_both(2, 1)
+    forward_both(3, 1)
+
+    m_ref[...] = jnp.full_like(m_ref, NEG)
+    l_ref[...] = jnp.zeros_like(l_ref)
+    acc_ref[...] = jnp.zeros_like(acc_ref)
     own_q.wait()
     for d in range(4):
         for dx in range(2):
             if d or dx:
-                block = qg.at[(y + d) % NY, (x + dx) % NX]
+                block = qg.at[(y + d) % NY, q_rows(x + dx)]
                 remote(block, block, q_send.at[d, dx], q_recv.at[d, dx], at(y + d, z, x + dx)).wait_recv()
-    for copy in sent:
-        copy.wait_send()
-
-
-def attend_kernel(kv, q, o, lse, m_ref, l_ref, acc_ref):
-    y, z, x = place()
-    tokens = kv.shape[3]
-    wide = 2 * tokens
-    keys = 2 * tokens
-    factor = SCALE * LOG2E
-
-    def block(yy, zp, queries, masked):
-        k = jnp.concatenate([kv[yy, 2 * zp, 0], kv[yy, 2 * zp + 1, 0]], axis=0)
-        v = jnp.concatenate([kv[yy, 2 * zp, 1], kv[yy, 2 * zp + 1, 1]], axis=0)
-        s = mm_nt(k, queries)
-        if masked:
-            row = lax.broadcasted_iota(jnp.int32, (keys, wide), 0)
-            col = lax.broadcasted_iota(jnp.int32, (keys, wide), 1)
-            key_at = zp * (4 * tokens) + x * tokens + row + jnp.where(row >= tokens, tokens, 0)
-            seen = key_at <= z * wide + col
-            s = jnp.where(seen, s, NEG)
-        old = m_ref[...]
-        new = jnp.maximum(old, jnp.max(s, axis=0, keepdims=True))
-        p = jnp.exp2((s - new) * factor)
-        if masked:
-            p = jnp.where(seen, p, 0.0)
-        shrink = jnp.exp2((old - new) * factor)
-        l_ref[...] = l_ref[...] * shrink + jnp.sum(p, axis=0, keepdims=True)
-        acc_ref[...] = acc_ref[...] * shrink + mm_tn(v, p)
-        m_ref[...] = new
-
-    for yq in range(NY):
-        queries = jnp.concatenate([q[yq, 0], q[yq, 1]], axis=0)
-        m_ref[...] = jnp.full_like(m_ref, NEG)
-        l_ref[...] = jnp.zeros_like(l_ref)
-        acc_ref[...] = jnp.zeros_like(acc_ref)
-
-        @pl.loop(0, yq * (NZ // 2))
-        def _(n):
-            block(n // (NZ // 2), n % (NZ // 2), queries, False)
-
-        @pl.loop(0, z // 2)
-        def _(n):
-            block(yq, n, queries, False)
-
-        block(yq, z // 2, queries, True)
-        total = l_ref[...]
+
+    def attend_later(yk, k, v):
+        for case in range(NY - 1):
+
+            @pl.when(yk == case)
+            def _():
+                attend(range(case + 1, NY), k(), v(), qg, m_ref, l_ref, acc_ref)
+
+    def attend_single(yk, zk):
+        attend_later(yk, lambda: kv[yk, zk, 0], lambda: kv[yk, zk, 1])
+
+    def attend_same(yk, zk):
+        @pl.when(zk < z)
+        def _():
+            attend([yk], kv[yk, zk, 0], kv[yk, zk, 1], qg, m_ref, l_ref, acc_ref)
+
+    @pl.loop(0, NY)
+    def _(j):
+        yk = y_of(j)
+        attend_single(yk, z)
+        key_at = lax.broadcasted_iota(jnp.int32, (tokens, wide), 0) + x * tokens
+        seen = key_at <= lax.broadcasted_iota(jnp.int32, (tokens, wide), 1)
+        attend([yk], kv[yk, z, 0], kv[yk, z, 1], qg, m_ref, l_ref, acc_ref, seen)
+
+    stages = {0: level_one, 4: level_two, 8: level_three}
+
+    @pl.loop(0, 12)
+    def _(n):
+        j, hop = n % NY, n // NY + 1
+        for when, stage in stages.items():
+            pl.when(n == when)(stage)
+        yk = y_of(j)
+        before, after = (z - hop + NZ) % NZ, (z + hop) % NZ
+        attend_later(
+            yk,
+            lambda: jnp.concatenate([kv[yk, before, 0], kv[yk, after, 0]], axis=0),
+            lambda: jnp.concatenate([kv[yk, before, 1], kv[yk, after, 1]], axis=0),
+        )
+        attend_same(yk, before)
+        attend_same(yk, after)
+
+        @pl.when((hop < 3) | (j < 2))
+        def _():
+            arrive_up(j, hop + 1)
+
+        @pl.when((hop == 1) | ((hop == 2) & (j < 2)))
+        def _():
+            upward(j, hop + 1).start()
+
+        @pl.when((hop < 3) | (j >= 2))
+        def _():
+            arrive_down(j, hop + 1)
+
+        @pl.when((hop == 1) | ((hop == 2) & (j >= 2)))
+        def _():
+            downward(j, hop + 1).start()
+
+    @pl.loop(0, NY)
+    def _(j):
+        yk = y_of(j)
+        attend_single(yk, (z + 4) % NZ)
+        attend_same(yk, (z + 4) % NZ)
+
+    for t in range(NY):
+        total = l_ref[t]
         some = total > 0.0
         safe = jnp.where(some, total, 1.0)
-        out = acc_ref[...] / safe
-        o[yq] = out.T.astype(BF16)
-        level = jnp.where(some, m_ref[...] * factor + jnp.log2(safe), NEG)
-        lse[yq] = jnp.broadcast_to(level, (8, wide))
+        o[t] = (acc_ref[t] / safe).T.astype(BF16)
+        level = jnp.where(some, m_ref[t] * (SCALE * LOG2E) + jnp.log2(safe), NEG)
+        lse[t] = jnp.broadcast_to(level, (8, wide))
+    states_in()
+    for copy in sent + exchange(1, t_buf, g, in_chain) + exchange(2, u_buf, y, in_column) + states_out():
+        copy.wait_send()
+    for j in range(NY):
+        for hop in range(4):
+            if hop < UP_HOPS[j]:
+                upward(j, hop).wait_send()
+            if hop < DOWN_HOPS[j]:
+                downward(j, hop).wait_send()
 
 
 def finish_kernel(
@@ -462,7 +523,7 @@
 VMEM = pl.BlockSpec(memory_space=pltpu.VMEM)
 ANY = pl.BlockSpec(memory_space=pl.ANY)
 DMA = pltpu.SemaphoreType.DMA
-LIMIT = 48 * 1024 * 1024
+LIMIT = 60 * 1024 * 1024
 
 
 def local(
@@ -471,27 +532,35 @@
 ):
     tokens, cols = delta_q.shape
     struct = jax.ShapeDtypeStruct
-    rows = jnp.concatenate(
-        [log_decay.T, resets.astype(F32)[None], jnp.zeros((3, tokens), F32)], axis=0
-    )
-    kv, qg, sin, oloc, qeff = pl.pallas_call(
-        gather_kernel,
+    wide = NX * tokens
+    vmem = pltpu.VMEM
+    o, lse, sin, oloc, qeff = pl.pallas_call(
+        main_kernel,
         out_shape=(
-            struct((NY, NZ, 2, tokens, HD), BF16),
-            struct((NY, NX, tokens, HD), BF16),
+            struct((NY, wide, HD), BF16),
+            struct((NY, 8, wide), F32),
             struct((HEADS, HD, HD), BF16),
             struct((tokens, cols), F32),
             struct((tokens, cols), BF16),
         ),
-        in_specs=[VMEM] * 8,
-        out_specs=(ANY, ANY, VMEM, VMEM, VMEM),
+        in_specs=[ANY] * 9,
+        out_specs=(VMEM,) * 5,
         scratch_shapes=[
-            pltpu.VMEM((HEADS, 2, HD, HD), BF16),
-            pltpu.VMEM((GROUP, 2, HD, HD), BF16),
-            pltpu.VMEM((GROUP, 2, HD, HD), BF16),
-            pltpu.VMEM((NY, 2, HD, HD), BF16),
-            pltpu.VMEM((4, 2, HD, HD), F32),
-            pltpu.VMEM((GROUP, HD, HD), BF16),
+            vmem((tokens, cols), BF16), vmem((tokens, cols), BF16), vmem((tokens, cols), BF16),
+            vmem((HEADS, tokens), F32), vmem((HEADS, tokens), F32), vmem((1, tokens), jnp.int32),
+            vmem((16, tokens), F32),
+            vmem((NY, NZ, 2, tokens, HD), BF16),
+            vmem((NY, wide, HD), BF16),
+            vmem((NY, 1, wide), F32),
+            vmem((NY, 1, wide), F32),
+            vmem((NY, HD, wide), F32),
+            vmem((HEADS, 2, HD, HD), BF16),
+            vmem((GROUP, 2, HD, HD), BF16),
+            vmem((GROUP, 2, HD, HD), BF16),
+            vmem((NY, 2, HD, HD), BF16),
+            vmem((4, 2, HD, HD), F32),
+            vmem((GROUP, HD, HD), BF16),
+            DMA((6,)),
             DMA((3,)),
             DMA((4, 2)), DMA((4, 2)),
             DMA((4, 2)), DMA((4, 2)),
@@ -502,19 +571,10 @@
         compiler_params=pltpu.CompilerParams(
             collective_id=0, has_side_effects=True, vmem_limit_bytes=LIMIT
         ),
-    )(delta_q, delta_k, delta_v, beta, rows, attn_q, attn_k, attn_v)
-    o, lse = pl.pallas_call(
-        attend_kernel,
-        out_shape=(struct((NY, NX * tokens, HD), BF16), struct((NY, 8, NX * tokens), F32)),
-        in_specs=[VMEM] * 2,
-        out_specs=(VMEM, VMEM),
-        scratch_shapes=[
-            pltpu.VMEM((1, NX * tokens), F32),
-            pltpu.VMEM((1, NX * tokens), F32),
-            pltpu.VMEM((HD, NX * tokens), F32),
-        ],
-        compiler_params=pltpu.CompilerParams(vmem_limit_bytes=LIMIT),
-    )(kv, qg)
+    )(
+        delta_q, delta_k, delta_v, beta.T, log_decay.T, resets.reshape(1, tokens),
+        attn_q, attn_k, attn_v,
+    )
     return pl.pallas_call(
         finish_kernel,
         out_shape=struct((tokens, cols), BF16),

time: 106 us -> 85.4 us (0.81)
  the two profiles are of different devices: /device:TPU:227 before, /device:TPU:193 now
where the time goes in v2:
time: 85.4 us; the launch traced here: 85.2 us
  Pallas kernels  83.6 us (98%)
  local copies, waits for them, and re-layouts  1.62 us (2%)
    pallas_call x1, Pallas kernels, local(): pl.pallas_call(main_kernel, out_shape=(struct((NY, wide, HD), BF16), stru...  56.6 us
    pallas_call x1, Pallas kernels, local(): pl.pallas_call(finish_kernel, out_shape=struct((tokens, cols), BF16), in_...  27 us

profile of v2, /device:TPU:193, one launch (start us, length us, event | category | flops | bytes accessed | tf_op | source)
XLA Modules:
  0.0 85.2 jit_solution(14628748149460430789)
XLA Ops:
  0.0 56.6 %shard_map.127 = (bf16[4,384,128]{2,1,0:T(8,128)(2,1)}, f32[4,8,384]{2,1,0:T(8,128)}, bf16[4,128,128]{2,1,0:T(8,128)(2,1)}, f32[192,512]{1,0:T(8,128)}, bf16[192,512]{1,0:T(8,128)(2,1)}) custom-call(bf16[192,512]{1,0:T(8,128)(2,1)} %dq_in.1, bf16[192,512]{1,0:T(8,128)(2,1)} %dk_in.1, bf16[192,512]{1,0:T(8,128)(2,1)} %dv_in.1, f32[4,192]{1,0:T(4,128)} %bitcast.5, ...), custom_call_target="tpu_custom_call" | custom-call | tf_op jit(solution)/shard_map/pallas_call | solution.py:537
  56.6 27.0 %shard_map.128 = bf16[192,512]{1,0:T(8,128)(2,1)} custom-call(bf16[4,384,128]{2,1,0:T(8,128)(2,1)} %get-tuple-element.10.o, f32[4,8,384]{2,1,0:T(8,128)} %get-tuple-element.11.lse, bf16[192,512]{1,0:T(8,128)(2,1)} %hidden.1, bf16[512,2048]{1,0:T(8,128)(2,1)} %weight.1, f32[192,512]{1,0:T(8,128)} %get-tuple-element.12.oloc, ...), custom_call_target="tpu_custom_call" | custom-call | tf_op jit(solution)/shard_map/pallas_call | solution.py:578
  83.6 1.6 %copy.15 = bf16[192,512]{1,0:T(8,128)(2,1)} copy(bf16[192,512]{1,0:T(8,128)(2,1)} %shard_map.128) | data formatting | bytes 393216

commit v3 on v2

--- a/solution.py
+++ b/solution.py
@@ -122,22 +122,31 @@
 
 
 def main_kernel(
-    dq_in, dk_in, dv_in, beta_in, decay_in, resets_in, aq, ak, av,
-    o, lse, sin, oloc, qeff,
+    dq_in, dk_in, dv_in, beta_in, decay_in, resets_in, aq, ak, av, weight, dgain_in, again_in,
+    out,
+    o, lse, sin, oloc, qeff, dgain, again, normed, o_recv, lse_recv, comb, wcol,
     dq, dk, dv, beta, decay, resets, rows,
     kv, qg, m_ref, l_ref, acc_ref,
     ab_send, ab_recv, t_buf, u_buf, e_buf, s_send,
     in_sem, own_sem, kv_send, kv_recv, q_send, q_recv, up_send, up_recv, down_send, down_recv,
     c_send, c_recv,
+    o_send_sem, o_recv_sem, l_send_sem, l_recv_sem, w_send, w_recv, ag_send, ag_recv, relay_send, relay_recv,
 ):
     y, z, x = place()
+    me = lax.axis_index("head")
+    sibling, facing = me + 1 - 2 * (me % 2), (me + 2) % 4
+    diagonal = (sibling + 2) % 4
+    cols = dq.shape[1]
     r, g = (z % 2) * 2 + x, z // 2
     tokens = dq.shape[0]
     wide = NX * tokens
     loads = [
         pltpu.make_async_copy(a, b, in_sem.at[i])
         for i, (a, b) in enumerate(
-            zip((dq_in, dk_in, dv_in, beta_in, decay_in, resets_in), (dq, dk, dv, beta, decay, resets))
+            zip(
+                (dq_in, dk_in, dv_in, beta_in, decay_in, resets_in, dgain_in, again_in),
+                (dq, dk, dv, beta, decay, resets, dgain, again),
+            )
         )
     ]
     for load in loads:
@@ -148,6 +157,7 @@
     peers += [at(y + d, z, x + 1) for d in range(4)]
     peers += [at(y, across, x), at(y, across, x + 1), at(y, beyond, x)]
     peers += [at(y, z + d, x) for d in (2, 4, 6)]
+    peers += [{"head": (me + d) % 4} for d in (1, 2, 3)]
     barrier = pltpu.get_barrier_semaphore()
     for peer in peers:
         pl.semaphore_signal(barrier, inc=1, device_id=peer, device_id_type=MESH)
@@ -337,7 +347,20 @@
             block = sin.at[(r - d + GROUP) % GROUP]
             remote(block, block, c_send.at[3, d], c_recv.at[3, d], of_group(r + 1)).wait_recv()
 
+    def weight_cols(device):
+        return weight.at[:, pl.ds(pl.multiple_of(device * cols, HD), cols)]
+
+    def weights_out():
+        own_w.start()
+        for d in (1, 2, 3):
+            to = (me + d) % 4
+            copy = remote(weight_cols(to), wcol.at[me], w_send.at[d], w_recv.at[d], {"head": to})
+            copy.start()
+            sent.append(copy)
+
+    own_w = pltpu.make_async_copy(weight_cols(me), wcol.at[me], own_sem.at[3])
     pairs_out()
+    weights_out()
     forward_both(2, 1)
     forward_both(3, 1)
 
@@ -368,13 +391,14 @@
 
     @pl.loop(0, NY)
     def _(j):
+        pl.when(j == 2)(level_one)
         yk = y_of(j)
         attend_single(yk, z)
         key_at = lax.broadcasted_iota(jnp.int32, (tokens, wide), 0) + x * tokens
         seen = key_at <= lax.broadcasted_iota(jnp.int32, (tokens, wide), 1)
         attend([yk], kv[yk, z, 0], kv[yk, z, 1], qg, m_ref, l_ref, acc_ref, seen)
 
-    stages = {0: level_one, 4: level_two, 8: level_three}
+    stages = {2: level_two, 6: level_three}
 
     @pl.loop(0, 12)
     def _(n):
@@ -383,6 +407,14 @@
             pl.when(n == when)(stage)
         yk = y_of(j)
         before, after = (z - hop + NZ) % NZ, (z + hop) % NZ
+
+        @pl.when(hop == 3)
+        def _():
+            arrive_up(j, 3)
+            pl.when(j < 2)(lambda: upward(j, 3).start())
+            arrive_down(j, 3)
+            pl.when(j >= 2)(lambda: downward(j, 3).start())
+
         attend_later(
             yk,
             lambda: jnp.concatenate([kv[yk, before, 0], kv[yk, after, 0]], axis=0),
@@ -391,36 +423,100 @@
         attend_same(yk, before)
         attend_same(yk, after)
 
-        @pl.when((hop < 3) | (j < 2))
+        @pl.when(hop == 1)
         def _():
-            arrive_up(j, hop + 1)
-
-        @pl.when((hop == 1) | ((hop == 2) & (j < 2)))
-        def _():
-            upward(j, hop + 1).start()
-
-        @pl.when((hop < 3) | (j >= 2))
-        def _():
-            arrive_down(j, hop + 1)
-
-        @pl.when((hop == 1) | ((hop == 2) & (j >= 2)))
-        def _():
-            downward(j, hop + 1).start()
+            forward_both(j, 2)
+
+    states_in()
+    for h in range(HEADS):
+        col = slice(h * HD, (h + 1) * HD)
+        raw = mm_nt(qeff[:, col], sin[h]) + oloc[:, col]
+        scaled = raw * lax.rsqrt(jnp.mean(raw * raw, axis=-1, keepdims=True) + EPSILON)
+        normed[h] = scaled * dgain[...]
 
     @pl.loop(0, NY)
     def _(j):
+        pl.when(j < 2)(lambda: arrive_up(j, 4))
+        pl.when(j >= 2)(lambda: arrive_down(j, 4))
         yk = y_of(j)
         attend_single(yk, (z + 4) % NZ)
         attend_same(yk, (z + 4) % NZ)
 
-    for t in range(NY):
+    for d in (2, 1, 3, 0):
+        t = (y + d) % NY
         total = l_ref[t]
         some = total > 0.0
         safe = jnp.where(some, total, 1.0)
         o[t] = (acc_ref[t] / safe).T.astype(BF16)
         level = jnp.where(some, m_ref[t] * (SCALE * LOG2E) + jnp.log2(safe), NEG)
         lse[t] = jnp.broadcast_to(level, (8, wide))
-    states_in()
+        for dx in range(2):
+            if d or dx:
+                to, back = at(t, z, x + dx), (NY - d) % NY
+                copy = remote(
+                    o.at[t, q_rows(x + dx)], o_recv.at[y, x], o_send_sem.at[d, dx], o_recv_sem.at[back, dx], to
+                )
+                copy.start()
+                sent.append(copy)
+                copy = remote(lse.at[t], lse_recv.at[y, x], l_send_sem.at[d, dx], l_recv_sem.at[back, dx], to)
+                copy.start()
+                sent.append(copy)
+    o_recv[y, x] = o[y, q_rows(x), :]
+    lse_recv[y, x] = lse[y]
+
+    pick = (
+        lax.broadcasted_iota(jnp.int32, (tokens, wide), 1)
+        == lax.broadcasted_iota(jnp.int32, (tokens, wide), 0) + x * tokens
+    ).astype(F32)
+    first_half = lax.broadcasted_iota(jnp.int32, (8, wide), 0) < 4
+
+    def piece_of(device, j):
+        return comb.at[device, :, head_cols(y_of(j))]
+
+    for j in range(NY):
+        d = Y_ORDER[j]
+        h = (y + d) % NY
+        for dx in range(2):
+            if d or dx:
+                there = (x + dx) % NX
+                block = o_recv.at[h, there]
+                remote(block, block, o_send_sem.at[d, dx], o_recv_sem.at[d, dx], at(h, z, there)).wait_recv()
+                block = lse_recv.at[h, there]
+                remote(block, block, l_send_sem.at[d, dx], l_recv_sem.at[d, dx], at(h, z, there)).wait_recv()
+        a, b = lse_recv[h, 0], lse_recv[h, 1]
+        top = jnp.maximum(a, b)
+        a, b = jnp.exp2(a - top), jnp.exp2(b - top)
+        shares = mm_nt(pick, jnp.where(first_half, a, b) / (a + b), HIGHEST)
+        raw = o_recv[h, 0].astype(F32) * shares[:, :1] + o_recv[h, 1].astype(F32) * shares[:, 4:5]
+        scaled = raw * lax.rsqrt(jnp.mean(raw * raw, axis=-1, keepdims=True) + EPSILON)
+        comb[me, :, head_cols(h)] = (0.5 * (normed[h] + scaled * again[...])).astype(BF16)
+        for way, to in enumerate((facing, sibling)):
+            copy = remote(piece_of(me, j), piece_of(me, j), ag_send.at[way, j], ag_recv.at[way, j], {"head": to})
+            copy.start()
+            sent.append(copy)
+
+    def share(device):
+        return jnp.dot(comb[device], wcol[device], preferred_element_type=F32)
+
+    for j in range(NY):
+        block = piece_of(facing, j)
+        remote(block, block, ag_send.at[0, j], ag_recv.at[0, j], {"head": facing}).wait_recv()
+        copy = remote(block, block, relay_send.at[j], relay_recv.at[j], {"head": sibling})
+        copy.start()
+        sent.append(copy)
+    own_w.wait()
+    for d in (1, 2, 3):
+        block = wcol.at[(me - d + 4) % 4]
+        remote(block, block, w_send.at[d], w_recv.at[d], {"head": (me + d) % 4}).wait_recv()
+    total = share(me) + share(facing)
+    for j in range(NY):
+        block = piece_of(sibling, j)
+        remote(block, block, ag_send.at[1, j], ag_recv.at[1, j], {"head": sibling}).wait_recv()
+    total = total + share(sibling)
+    for j in range(NY):
+        block = piece_of(diagonal, j)
+        remote(block, block, relay_send.at[j], relay_recv.at[j], {"head": sibling}).wait_recv()
+    out[...] = total + share(diagonal)
     for copy in sent + exchange(1, t_buf, g, in_chain) + exchange(2, u_buf, y, in_column) + states_out():
         copy.wait_send()
     for j in range(NY):
@@ -431,95 +527,6 @@
                 downward(j, hop).wait_send()
 
 
-def finish_kernel(
-    o, lse, hidden, weight, oloc, qeff, sin, dgain, again,
-    out,
-    o_recv, lse_recv, part, part_recv,
-    o_send_sem, o_recv_sem, l_send_sem, l_recv_sem, w_send_sem, w_recv_sem,
-):
-    y, z, x = place()
-    me = lax.axis_index("head")
-    tokens, cols = hidden.shape
-    others = [(d, dx) for d in range(4) for dx in range(2) if d or dx]
-    barrier = pltpu.get_barrier_semaphore()
-    for d, dx in others:
-        pl.semaphore_signal(barrier, inc=1, device_id=at(y + d, z, x + dx), device_id_type=MESH)
-    for d in (1, 2, 3):
-        pl.semaphore_signal(barrier, inc=1, device_id={"head": (me + d) % 4}, device_id_type=MESH)
-    pl.semaphore_wait(barrier, len(others) + 3)
-    sent = []
-    for d, dx in others:
-        ty, tx = (y + d) % NY, (x + dx) % NX
-        rows = pl.ds(pl.multiple_of(tx * tokens, 64), tokens)
-        copy = remote(
-            o.at[ty, rows], o_recv.at[y, x],
-            o_send_sem.at[d, dx], o_recv_sem.at[(NY - d) % NY, dx], at(ty, z, tx),
-        )
-        copy.start()
-        sent.append(copy)
-        copy = remote(
-            lse.at[ty], lse_recv.at[y, x],
-            l_send_sem.at[d, dx], l_recv_sem.at[(NY - d) % NY, dx], at(ty, z, tx),
-        )
-        copy.start()
-        sent.append(copy)
-    o_recv[y, x] = o[y, pl.ds(pl.multiple_of(x * tokens, 64), tokens), :]
-    lse_recv[y, x] = lse[y]
-
-    delta = []
-    for h in range(HEADS):
-        col = slice(h * HD, (h + 1) * HD)
-        raw = mm_nt(qeff[:, col], sin[h]) + oloc[:, col]
-        scaled = raw * lax.rsqrt(jnp.mean(raw * raw, axis=-1, keepdims=True) + EPSILON)
-        delta.append(scaled * dgain[...])
-
-    for d, dx in others:
-        block = o_recv.at[(y + d) % NY, (x + dx) % NX]
-        remote(block, block, o_send_sem.at[d, dx], o_recv_sem.at[d, dx], at(y + d, z, x + dx)).wait_recv()
-        block = lse_recv.at[(y + d) % NY, (x + dx) % NX]
-        remote(block, block, l_send_sem.at[d, dx], l_recv_sem.at[d, dx], at(y + d, z, x + dx)).wait_recv()
-
-    shares = []
-    for h in range(HEADS):
-        a, b = lse_recv[h, 0][:1], lse_recv[h, 1][:1]
-        top = jnp.maximum(a, b)
-        a, b = jnp.exp2(a - top), jnp.exp2(b - top)
-        both = a + b
-        shares += [a / both, b / both]
-    shares = jnp.concatenate(shares, axis=0)
-    pick = (
-        lax.broadcasted_iota(jnp.int32, (tokens, 2 * tokens), 1)
-        == lax.broadcasted_iota(jnp.int32, (tokens, 2 * tokens), 0) + x * tokens
-    ).astype(F32)
-    shares = mm_nt(pick, shares, HIGHEST)
-    combined = []
-    for h in range(HEADS):
-        raw = (
-            o_recv[h, 0].astype(F32) * shares[:, 2 * h : 2 * h + 1]
-            + o_recv[h, 1].astype(F32) * shares[:, 2 * h + 1 : 2 * h + 2]
-        )
-        scaled = raw * lax.rsqrt(jnp.mean(raw * raw, axis=-1, keepdims=True) + EPSILON)
-        combined.append((0.5 * (delta[h] + scaled * again[...])).astype(BF16))
-    combined = jnp.concatenate(combined, axis=1)
-    for d in (1, 2, 3):
-        to = (me + d) % 4
-        columns = pl.ds(pl.multiple_of(to * cols, HD), cols)
-        part[d] = jnp.dot(combined, weight[:, columns], preferred_element_type=F32).astype(BF16)
-        copy = remote(part.at[d], part_recv.at[d], w_send_sem.at[d], w_recv_sem.at[d], {"head": to})
-        copy.start()
-        sent.append(copy)
-    total = jnp.dot(
-        combined, weight[:, pl.ds(pl.multiple_of(me * cols, HD), cols)], preferred_element_type=F32
-    )
-    for d in (1, 2, 3):
-        block = part_recv.at[d]
-        remote(block, block, w_send_sem.at[d], w_recv_sem.at[d], {"head": (me + d) % 4}).wait_recv()
-        total = total + part_recv[d].astype(F32)
-    out[...] = (hidden[...].astype(F32) + total).astype(BF16)
-    for copy in sent:
-        copy.wait_send()
-
-
 VMEM = pl.BlockSpec(memory_space=pltpu.VMEM)
 ANY = pl.BlockSpec(memory_space=pl.ANY)
 DMA = pltpu.SemaphoreType.DMA
@@ -534,18 +541,24 @@
     struct = jax.ShapeDtypeStruct
     wide = NX * tokens
     vmem = pltpu.VMEM
-    o, lse, sin, oloc, qeff = pl.pallas_call(
+    shared = pl.pallas_call(
         main_kernel,
-        out_shape=(
-            struct((NY, wide, HD), BF16),
-            struct((NY, 8, wide), F32),
-            struct((HEADS, HD, HD), BF16),
-            struct((tokens, cols), F32),
-            struct((tokens, cols), BF16),
-        ),
-        in_specs=[ANY] * 9,
-        out_specs=(VMEM,) * 5,
+        out_shape=struct((tokens, cols), F32),
+        in_specs=[ANY] * 12,
+        out_specs=VMEM,
         scratch_shapes=[
+            vmem((NY, wide, HD), BF16),
+            vmem((NY, 8, wide), F32),
+            vmem((HEADS, HD, HD), BF16),
+            vmem((tokens, cols), F32),
+            vmem((tokens, cols), BF16),
+            vmem((1, HD), F32),
+            vmem((1, HD), F32),
+            vmem((HEADS, tokens, HD), F32),
+            vmem((NY, NX, tokens, HD), BF16),
+            vmem((NY, NX, 8, wide), F32),
+            vmem((4, tokens, cols), BF16),
+            vmem((4, cols, cols), BF16),
             vmem((tokens, cols), BF16), vmem((tokens, cols), BF16), vmem((tokens, cols), BF16),
             vmem((HEADS, tokens), F32), vmem((HEADS, tokens), F32), vmem((1, tokens), jnp.int32),
             vmem((16, tokens), F32),
@@ -560,42 +573,28 @@
             vmem((NY, 2, HD, HD), BF16),
             vmem((4, 2, HD, HD), F32),
             vmem((GROUP, HD, HD), BF16),
-            DMA((6,)),
-            DMA((3,)),
+            DMA((8,)),
+            DMA((4,)),
             DMA((4, 2)), DMA((4, 2)),
             DMA((4, 2)), DMA((4, 2)),
             DMA((4, 4)), DMA((4, 4)),
             DMA((4, 4)), DMA((4, 4)),
             DMA((4, 4)), DMA((4, 4)),
+            DMA((4, 2)), DMA((4, 2)),
+            DMA((4, 2)), DMA((4, 2)),
+            DMA((4,)), DMA((4,)),
+            DMA((2, 4)), DMA((2, 4)),
+            DMA((4,)), DMA((4,)),
         ],
         compiler_params=pltpu.CompilerParams(
             collective_id=0, has_side_effects=True, vmem_limit_bytes=LIMIT
         ),
     )(
         delta_q, delta_k, delta_v, beta.T, log_decay.T, resets.reshape(1, tokens),
-        attn_q, attn_k, attn_v,
-    )
-    return pl.pallas_call(
-        finish_kernel,
-        out_shape=struct((tokens, cols), BF16),
-        in_specs=[VMEM] * 9,
-        out_specs=VMEM,
-        scratch_shapes=[
-            pltpu.VMEM((NY, NX, tokens, HD), BF16),
-            pltpu.VMEM((NY, NX, 8, NX * tokens), F32),
-            pltpu.VMEM((4, tokens, cols), BF16),
-            pltpu.VMEM((4, tokens, cols), BF16),
-            DMA((4, 2)), DMA((4, 2)),
-            DMA((4, 2)), DMA((4, 2)),
-            DMA((4,)), DMA((4,)),
-        ],
-        compiler_params=pltpu.CompilerParams(
-            collective_id=1, has_side_effects=True, vmem_limit_bytes=LIMIT
-        ),
-    )(
-        o, lse, hidden_in, out_weight, oloc, qeff, sin,
+        attn_q, attn_k, attn_v, out_weight,
         delta_gain.reshape(1, HD), attn_gain.reshape(1, HD),
     )
+    return (hidden_in.astype(F32) + shared).astype(BF16)
 
 
 def solution(mesh):

time: 85.4 us -> 79.8 us (0.934)
  the two profiles are of different devices: /device:TPU:193 before, /device:TPU:25 now
where the time goes in v3:
time: 79.8 us; the launch traced here: 78.3 us
  Pallas kernels  76.6 us (96%)
  other arithmetic  1.71 us (2%)
    pallas_call x1, Pallas kernels, local(): pl.pallas_call(main_kernel, out_shape=struct((tokens, cols), F32), in_spe...  76.6 us
    convert_element_type x1, other arithmetic, local(): return (hidden_in.astype(F32) + shared).astype(BF16)  1.71 us

profile of v3, /device:TPU:25, one launch (start us, length us, event | category | flops | bytes accessed | tf_op | source)
XLA Modules:
  0.0 78.3 jit_solution(17671064254744436426)
XLA Ops:
  0.0 0.0 copy-start
  0.0 76.6 %shard_map.127 = f32[192,512]{1,0:T(8,128)} custom-call(bf16[192,512]{1,0:T(8,128)(2,1)} %dq_in.1, bf16[192,512]{1,0:T(8,128)(2,1)} %dk_in.1, bf16[192,512]{1,0:T(8,128)(2,1)} %dv_in.1, f32[4,192]{1,0:T(4,128)} %bitcast.5, f32[4,192]{1,0:T(4,128)} %bitcast.6, s32[1,192]{1,0:T(1,128)} %bitcast.7, bf16[192,512]{1,0:T(8,128)(2,1)} %aq.1, bf16[192,512]{1,0:T(8,128)(2,1)} %ak.1, ...), custom_call_target="tpu_custom_call" | custom-call | tf_op jit(solution)/shard_map/pallas_call | solution.py:544
  76.6 0.0 copy-done
  76.6 1.7 %add_convert_fusion = bf16[192,512]{1,0:T(8,128)(2,1)} fusion(f32[192,512]{1,0:T(8,128)} %shard_map.127, bf16[192,512]{1,0:T(8,128)(2,1)S(1)} %copy-done), kind=kLoop, calls=%fused_computation | loop fusion | flops 294912 | bytes 786432 | tf_op jit(solution)/shard_map/convert_element_type | solution.py:597
Async XLA Ops:
  0.0 76.6 %copy-start = (bf16[192,512]{1,0:T(8,128)(2,1)S(1)}, bf16[192,512]{1,0:T(8,128)(2,1)}, u32[]{:S(2)}) copy-start(bf16[192,512]{1,0:T(8,128)(2,1)} %param.13) | copy-start | bytes 589828

commit v4 on v3

--- a/solution.py
+++ b/solution.py
@@ -104,21 +104,23 @@
     qeff[:, col] = (reach * q - seen[:, HD:]).astype(BF16)
 
 
-def attend(tiles, k, v, q, m_ref, l_ref, acc_ref, seen=None):
+def attend(first, tiles, k, v, q, m_ref, l_ref, acc_ref, seen=None):
     factor = SCALE * LOG2E
-    scores = [mm_nt(k, q[t]) for t in tiles]
-    for t, s in zip(tiles, scores):
-        if seen is not None:
-            s = jnp.where(seen, s, NEG)
-        old = m_ref[t]
-        new = jnp.maximum(old, jnp.max(s, axis=0, keepdims=True))
-        p = jnp.exp2((s - new) * factor)
-        if seen is not None:
-            p = jnp.where(seen, p, 0.0)
-        shrink = jnp.exp2((old - new) * factor)
-        l_ref[t] = l_ref[t] * shrink + jnp.sum(p, axis=0, keepdims=True)
-        acc_ref[t] = acc_ref[t] * shrink + mm_tn(v, p)
-        m_ref[t] = new
+    wide = q.shape[1] // NY
+    span = tiles * wide
+    at_ = pl.ds(first * wide, span) if isinstance(first, int) else pl.ds(pl.multiple_of(first * wide, HD), span)
+    s = jnp.dot(k, q[:, at_], preferred_element_type=F32)
+    if seen is not None:
+        s = jnp.where(seen, s, NEG)
+    old = m_ref[:, at_]
+    new = jnp.maximum(old, jnp.max(s, axis=0, keepdims=True))
+    p = jnp.exp2((s - new) * factor)
+    if seen is not None:
+        p = jnp.where(seen, p, 0.0)
+    shrink = jnp.exp2((old - new) * factor)
+    l_ref[:, at_] = l_ref[:, at_] * shrink + jnp.sum(p, axis=0, keepdims=True)
+    acc_ref[:, at_] = acc_ref[:, at_] * shrink + mm_tn(v, p)
+    m_ref[:, at_] = new
 
 
 def main_kernel(
@@ -126,7 +128,7 @@
     out,
     o, lse, sin, oloc, qeff, dgain, again, normed, o_recv, lse_recv, comb, wcol,
     dq, dk, dv, beta, decay, resets, rows,
-    kv, qg, m_ref, l_ref, acc_ref,
+    kv, qg, qt, m_ref, l_ref, acc_ref,
     ab_send, ab_recv, t_buf, u_buf, e_buf, s_send,
     in_sem, own_sem, kv_send, kv_recv, q_send, q_recv, up_send, up_recv, down_send, down_recv,
     c_send, c_recv,
@@ -173,6 +175,11 @@
     own_k = pltpu.make_async_copy(ak.at[:, head_cols(y)], kv.at[y, z, 0], own_sem.at[0])
     own_v = pltpu.make_async_copy(av.at[:, head_cols(y)], kv.at[y, z, 1], own_sem.at[1])
     own_q = pltpu.make_async_copy(aq.at[:, head_cols(y)], qg.at[y, q_rows(x)], own_sem.at[2])
+    for send, recv, dz in ((up_send, up_recv, 1), (down_send, down_recv, NZ - 1)):
+        for part, source in enumerate((ak, av)):
+            remote(
+                source.at[:, head_cols(y)], kv.at[y, z, part], send.at[0, 0], recv.at[0, 0], at(y, z + dz, x)
+            ).start()
     own_k.start()
     own_v.start()
     for j in (1, 2, 3):
@@ -205,10 +212,6 @@
         block = kv.at[y_of(j), (z + hop) % NZ]
         remote(block, block, down_send.at[j, hop - 1], down_recv.at[j, hop - 1], at(y, z + 1, x)).wait_recv()
 
-    own_k.wait()
-    own_v.wait()
-    upward(0, 0).start()
-    downward(0, 0).start()
     own_q.start()
     for d in range(4):
         for dx in range(2):
@@ -247,23 +250,20 @@
         arrive_down(j, hop)
         downward(j, hop).start()
 
+    def of_group(index):
+        return at(y, g * 2 + (index % GROUP) // 2, (index % GROUP) % 2)
+
+    def pair_copy(h):
+        d = (h - r + GROUP) % GROUP
+        return remote(ab_send.at[h], ab_recv.at[r], c_send.at[0, d], c_recv.at[0, d], of_group(h))
+
     for h in range(HEADS):
         delta_head(h, dq, dk, dv, betas, cum_col, cum_row, oloc, qeff, ab_send)
+        pl.when(r != h)(lambda: pair_copy(h).start())
         if h:
             first_round(h)
         if h >= 2:
             forward_both(h - 2, 1)
-
-    def of_group(index):
-        return at(y, g * 2 + (index % GROUP) // 2, (index % GROUP) % 2)
-
-    def pairs_out():
-        for d in (1, 2, 3):
-            to = (r + d) % GROUP
-            copy = remote(ab_send.at[to], ab_recv.at[r], c_send.at[0, d], c_recv.at[0, d], of_group(to))
-            copy.start()
-            sent.append(copy)
-        ab_recv[r] = ab_send[r]
 
     def pairs_in():
         for d in (1, 2, 3):
@@ -282,13 +282,16 @@
             remote(block, block, c_send.at[level, d], c_recv.at[level, d], device(d)).wait_recv()
 
     def fold(buf):
-        before = []
-        a, b = buf[0, 0].astype(F32), buf[0, 1].astype(F32)
-        for i in range(1, GROUP):
-            before.append((a, b))
-            both = mm(jnp.concatenate([a, b], axis=0), buf[i, 0])
-            a, b = both[:HD], both[HD:] + buf[i, 1].astype(F32)
-        return before, (a, b)
+        a, b = [buf[i, 0] for i in range(GROUP)], [buf[i, 1].astype(F32) for i in range(GROUP)]
+
+        def join(one, two):
+            both = mm(jnp.concatenate([one[0].astype(BF16), one[1].astype(BF16)], axis=0), two[0])
+            return both[:HD], both[HD:] + two[1]
+
+        pairs = list(zip(a, b))
+        early, late = join(pairs[0], pairs[1]), join(pairs[2], pairs[3])
+        first = (a[0].astype(F32), b[0])
+        return [first, early, join(early, pairs[2])], join(early, late)
 
     in_chain = lambda d: at(y, z + 2 * d, x)
     in_column = lambda d: at(y + d, z, x)
@@ -359,7 +362,7 @@
             sent.append(copy)
 
     own_w = pltpu.make_async_copy(weight_cols(me), wcol.at[me], own_sem.at[3])
-    pairs_out()
+    ab_recv[r] = ab_send[r]
     weights_out()
     forward_both(2, 1)
     forward_both(3, 1)
@@ -367,6 +370,8 @@
     m_ref[...] = jnp.full_like(m_ref, NEG)
     l_ref[...] = jnp.zeros_like(l_ref)
     acc_ref[...] = jnp.zeros_like(acc_ref)
+    own_k.wait()
+    own_v.wait()
     own_q.wait()
     for d in range(4):
         for dx in range(2):
@@ -374,12 +379,15 @@
                 block = qg.at[(y + d) % NY, q_rows(x + dx)]
                 remote(block, block, q_send.at[d, dx], q_recv.at[d, dx], at(y + d, z, x + dx)).wait_recv()
 
+    for t in range(NY):
+        qt[:, t * wide : (t + 1) * wide] = qg[t].T
+
     def attend_later(yk, k, v):
         for case in range(NY - 1):
 
             @pl.when(yk == case)
             def _():
-                attend(range(case + 1, NY), k(), v(), qg, m_ref, l_ref, acc_ref)
+                attend(case + 1, NY - 1 - case, k(), v(), qt, m_ref, l_ref, acc_ref)
 
     def attend_single(yk, zk):
         attend_later(yk, lambda: kv[yk, zk, 0], lambda: kv[yk, zk, 1])
@@ -387,18 +395,17 @@
     def attend_same(yk, zk):
         @pl.when(zk < z)
         def _():
-            attend([yk], kv[yk, zk, 0], kv[yk, zk, 1], qg, m_ref, l_ref, acc_ref)
+            attend(yk, 1, kv[yk, zk, 0], kv[yk, zk, 1], qt, m_ref, l_ref, acc_ref)
 
     @pl.loop(0, NY)
     def _(j):
-        pl.when(j == 2)(level_one)
         yk = y_of(j)
         attend_single(yk, z)
         key_at = lax.broadcasted_iota(jnp.int32, (tokens, wide), 0) + x * tokens
         seen = key_at <= lax.broadcasted_iota(jnp.int32, (tokens, wide), 1)
-        attend([yk], kv[yk, z, 0], kv[yk, z, 1], qg, m_ref, l_ref, acc_ref, seen)
-
-    stages = {2: level_two, 6: level_three}
+        attend(yk, 1, kv[yk, z, 0], kv[yk, z, 1], qt, m_ref, l_ref, acc_ref, seen)
+
+    stages = {0: level_one, 6: level_two, 9: level_three}
 
     @pl.loop(0, 12)
     def _(n):
@@ -427,13 +434,6 @@
         def _():
             forward_both(j, 2)
 
-    states_in()
-    for h in range(HEADS):
-        col = slice(h * HD, (h + 1) * HD)
-        raw = mm_nt(qeff[:, col], sin[h]) + oloc[:, col]
-        scaled = raw * lax.rsqrt(jnp.mean(raw * raw, axis=-1, keepdims=True) + EPSILON)
-        normed[h] = scaled * dgain[...]
-
     @pl.loop(0, NY)
     def _(j):
         pl.when(j < 2)(lambda: arrive_up(j, 4))
@@ -444,11 +444,12 @@
 
     for d in (2, 1, 3, 0):
         t = (y + d) % NY
-        total = l_ref[t]
+        tile = pl.ds(pl.multiple_of(t * wide, HD), wide)
+        total = l_ref[:, tile]
         some = total > 0.0
         safe = jnp.where(some, total, 1.0)
-        o[t] = (acc_ref[t] / safe).T.astype(BF16)
-        level = jnp.where(some, m_ref[t] * (SCALE * LOG2E) + jnp.log2(safe), NEG)
+        o[t] = (acc_ref[:, tile] * (1.0 / safe)).T.astype(BF16)
+        level = jnp.where(some, m_ref[:, tile] * (SCALE * LOG2E) + jnp.log2(safe), NEG)
         lse[t] = jnp.broadcast_to(level, (8, wide))
         for dx in range(2):
             if d or dx:
@@ -464,10 +465,13 @@
     o_recv[y, x] = o[y, q_rows(x), :]
     lse_recv[y, x] = lse[y]
 
-    pick = (
-        lax.broadcasted_iota(jnp.int32, (tokens, wide), 1)
-        == lax.broadcasted_iota(jnp.int32, (tokens, wide), 0) + x * tokens
-    ).astype(F32)
+    states_in()
+    for h in range(HEADS):
+        col = slice(h * HD, (h + 1) * HD)
+        raw = mm_nt(qeff[:, col], sin[h]) + oloc[:, col]
+        scaled = raw * lax.rsqrt(jnp.mean(raw * raw, axis=-1, keepdims=True) + EPSILON)
+        normed[h] = scaled * dgain[...]
+
     first_half = lax.broadcasted_iota(jnp.int32, (8, wide), 0) < 4
 
     def piece_of(device, j):
@@ -486,7 +490,8 @@
         a, b = lse_recv[h, 0], lse_recv[h, 1]
         top = jnp.maximum(a, b)
         a, b = jnp.exp2(a - top), jnp.exp2(b - top)
-        shares = mm_nt(pick, jnp.where(first_half, a, b) / (a + b), HIGHEST)
+        shares = (jnp.where(first_half, a, b) / (a + b)).T
+        shares = jnp.where(x == 0, shares[:tokens], shares[tokens:])
         raw = o_recv[h, 0].astype(F32) * shares[:, :1] + o_recv[h, 1].astype(F32) * shares[:, 4:5]
         scaled = raw * lax.rsqrt(jnp.mean(raw * raw, axis=-1, keepdims=True) + EPSILON)
         comb[me, :, head_cols(h)] = (0.5 * (normed[h] + scaled * again[...])).astype(BF16)
@@ -517,6 +522,8 @@
         block = piece_of(diagonal, j)
         remote(block, block, relay_send.at[j], relay_recv.at[j], {"head": sibling}).wait_recv()
     out[...] = total + share(diagonal)
+    for d in (1, 2, 3):
+        pair_copy((r + d) % GROUP).wait_send()
     for copy in sent + exchange(1, t_buf, g, in_chain) + exchange(2, u_buf, y, in_column) + states_out():
         copy.wait_send()
     for j in range(NY):
@@ -564,9 +571,10 @@
             vmem((16, tokens), F32),
             vmem((NY, NZ, 2, tokens, HD), BF16),
             vmem((NY, wide, HD), BF16),
-            vmem((NY, 1, wide), F32),
-            vmem((NY, 1, wide), F32),
-            vmem((NY, HD, wide), F32),
+            vmem((HD, NY * wide), BF16),
+            vmem((1, NY * wide), F32),
+            vmem((1, NY * wide), F32),
+            vmem((HD, NY * wide), F32),
             vmem((HEADS, 2, HD, HD), BF16),
             vmem((GROUP, 2, HD, HD), BF16),
             vmem((GROUP, 2, HD, HD), BF16),

time: 79.8 us -> 76.7 us (0.961)
  Pallas kernels: 76.6 us -> 73.5 us
    pallas_call x1, Pallas kernels: 76.6 us -> 73.5 us  [local(): pl.pallas_call(main_kernel, out_shape=struct((tokens, cols), F32), in_spe...]
where the time goes in v4:
time: 76.7 us; the launch traced here: 75.2 us
  Pallas kernels  73.5 us (96%)
  other arithmetic  1.71 us (2%)
    pallas_call x1, Pallas kernels, local(): pl.pallas_call(main_kernel, out_shape=struct((tokens, cols), F32), in_spe...  73.5 us
    convert_element_type x1, other arithmetic, local(): return (hidden_in.astype(F32) + shared).astype(BF16)  1.71 us

profile of v4, /device:TPU:25, one launch (start us, length us, event | category | flops | bytes accessed | tf_op | source)
XLA Modules:
  0.0 75.2 jit_solution(2468371230022745632)
XLA Ops:
  0.0 0.0 copy-start
  0.0 73.5 %shard_map.127 = f32[192,512]{1,0:T(8,128)} custom-call(bf16[192,512]{1,0:T(8,128)(2,1)} %dq_in.1, bf16[192,512]{1,0:T(8,128)(2,1)} %dk_in.1, bf16[192,512]{1,0:T(8,128)(2,1)} %dv_in.1, f32[4,192]{1,0:T(4,128)} %bitcast.5, f32[4,192]{1,0:T(4,128)} %bitcast.6, s32[1,192]{1,0:T(1,128)} %bitcast.7, bf16[192,512]{1,0:T(8,128)(2,1)} %aq.1, bf16[192,512]{1,0:T(8,128)(2,1)} %ak.1, ...), custom_call_target="tpu_custom_call" | custom-call | tf_op jit(solution)/shard_map/pallas_call | solution.py:551
  73.5 0.0 copy-done
  73.5 1.7 %add_convert_fusion = bf16[192,512]{1,0:T(8,128)(2,1)} fusion(f32[192,512]{1,0:T(8,128)} %shard_map.127, bf16[192,512]{1,0:T(8,128)(2,1)S(1)} %copy-done), kind=kLoop, calls=%fused_computation | loop fusion | flops 294912 | bytes 786432 | tf_op jit(solution)/shard_map/convert_element_type | solution.py:605
Async XLA Ops:
  0.0 73.5 %copy-start = (bf16[192,512]{1,0:T(8,128)(2,1)S(1)}, bf16[192,512]{1,0:T(8,128)(2,1)}, u32[]{:S(2)}) copy-start(bf16[192,512]{1,0:T(8,128)(2,1)} %param.13) | copy-start | bytes 589828

commit v5 on v4

--- a/solution.py
+++ b/solution.py
@@ -19,8 +19,8 @@
 SCALE = HD**-0.5
 LOG2E = 1.4426950408889634
 Y_ORDER = (0, 1, 3, 2)
-UP_HOPS = (4, 4, 3, 3)
-DOWN_HOPS = (3, 3, 4, 4)
+UP_HOPS = (4, 3, 4, 3)
+DOWN_HOPS = (3, 4, 3, 4)
 
 
 def mm(a, b):
@@ -178,7 +178,7 @@
     for send, recv, dz in ((up_send, up_recv, 1), (down_send, down_recv, NZ - 1)):
         for part, source in enumerate((ak, av)):
             remote(
-                source.at[:, head_cols(y)], kv.at[y, z, part], send.at[0, 0], recv.at[0, 0], at(y, z + dz, x)
+                source.at[:, head_cols(y)], kv.at[y, z, part], send.at[y, 0], recv.at[y, 0], at(y, z + dz, x)
             ).start()
     own_k.start()
     own_v.start()
@@ -193,23 +193,22 @@
             sent.append(copy)
 
     def y_of(j):
-        step = Y_ORDER[j] if isinstance(j, int) else j + jnp.where(j == 2, 1, 0) - jnp.where(j == 3, 1, 0)
-        return (y + step) % NY
+        return (y + Y_ORDER[j]) % NY
 
     def upward(j, hop):
-        block = kv.at[y_of(j), (z - hop + NZ) % NZ]
+        block = kv.at[j, (z - hop + NZ) % NZ]
         return remote(block, block, up_send.at[j, hop], up_recv.at[j, hop], at(y, z + 1, x))
 
     def downward(j, hop):
-        block = kv.at[y_of(j), (z + hop) % NZ]
+        block = kv.at[j, (z + hop) % NZ]
         return remote(block, block, down_send.at[j, hop], down_recv.at[j, hop], at(y, z - 1 + NZ, x))
 
     def arrive_up(j, hop):
-        block = kv.at[y_of(j), (z - hop + NZ) % NZ]
+        block = kv.at[j, (z - hop + NZ) % NZ]
         remote(block, block, up_send.at[j, hop - 1], up_recv.at[j, hop - 1], at(y, z + 1, x)).wait_recv()
 
     def arrive_down(j, hop):
-        block = kv.at[y_of(j), (z + hop) % NZ]
+        block = kv.at[j, (z + hop) % NZ]
         remote(block, block, down_send.at[j, hop - 1], down_recv.at[j, hop - 1], at(y, z + 1, x)).wait_recv()
 
     own_q.start()
@@ -241,8 +240,8 @@
         for part in range(2):
             block = kv.at[y_of(j), z, part]
             remote(block, block, kv_send.at[j, part], kv_recv.at[j, part], at(y + 1, z, x)).wait_recv()
-        upward(j, 0).start()
-        downward(j, 0).start()
+        upward(y_of(j), 0).start()
+        downward(y_of(j), 0).start()
 
     def forward_both(j, hop):
         arrive_up(j, hop)
@@ -262,8 +261,6 @@
         pl.when(r != h)(lambda: pair_copy(h).start())
         if h:
             first_round(h)
-        if h >= 2:
-            forward_both(h - 2, 1)
 
     def pairs_in():
         for d in (1, 2, 3):
@@ -364,8 +361,8 @@
     own_w = pltpu.make_async_copy(weight_cols(me), wcol.at[me], own_sem.at[3])
     ab_recv[r] = ab_send[r]
     weights_out()
-    forward_both(2, 1)
-    forward_both(3, 1)
+    for yk in range(NY):
+        forward_both(yk, 1)
 
     m_ref[...] = jnp.full_like(m_ref, NEG)
     l_ref[...] = jnp.zeros_like(l_ref)
@@ -398,8 +395,7 @@
             attend(yk, 1, kv[yk, zk, 0], kv[yk, zk, 1], qt, m_ref, l_ref, acc_ref)
 
     @pl.loop(0, NY)
-    def _(j):
-        yk = y_of(j)
+    def _(yk):
         attend_single(yk, z)
         key_at = lax.broadcasted_iota(jnp.int32, (tokens, wide), 0) + x * tokens
         seen = key_at <= lax.broadcasted_iota(jnp.int32, (tokens, wide), 1)
@@ -409,18 +405,17 @@
 
     @pl.loop(0, 12)
     def _(n):
-        j, hop = n % NY, n // NY + 1
+        yk, hop = n % NY, n // NY + 1
         for when, stage in stages.items():
             pl.when(n == when)(stage)
-        yk = y_of(j)
         before, after = (z - hop + NZ) % NZ, (z + hop) % NZ
 
         @pl.when(hop == 3)
         def _():
-            arrive_up(j, 3)
-            pl.when(j < 2)(lambda: upward(j, 3).start())
-            arrive_down(j, 3)
-            pl.when(j >= 2)(lambda: downward(j, 3).start())
+            arrive_up(yk, 3)
+            pl.when(yk % 2 == 0)(lambda: upward(yk, 3).start())
+            arrive_down(yk, 3)
+            pl.when(yk % 2 == 1)(lambda: downward(yk, 3).start())
 
         attend_later(
             yk,
@@ -432,36 +427,39 @@
 
         @pl.when(hop == 1)
         def _():
-            forward_both(j, 2)
-
-    @pl.loop(0, NY)
-    def _(j):
-        pl.when(j < 2)(lambda: arrive_up(j, 4))
-        pl.when(j >= 2)(lambda: arrive_down(j, 4))
-        yk = y_of(j)
-        attend_single(yk, (z + 4) % NZ)
-        attend_same(yk, (z + 4) % NZ)
-
-    for d in (2, 1, 3, 0):
-        t = (y + d) % NY
-        tile = pl.ds(pl.multiple_of(t * wide, HD), wide)
+            forward_both(yk, 2)
+
+    def tile_copies(t):
+        d = (t - y + NY) % NY
+        for xx in range(NX):
+            dx, to, back = (xx - x + NX) % NX, at(t, z, xx), (NY - d) % NY
+            rows_of = slice(xx * tokens, (xx + 1) * tokens)
+            elsewhere = (t != y) | (xx != x)
+            yield elsewhere, (
+                remote(o.at[t, rows_of], o_recv.at[y, x], o_send_sem.at[d, dx], o_recv_sem.at[back, dx], to),
+                remote(lse.at[t], lse_recv.at[y, x], l_send_sem.at[d, dx], l_recv_sem.at[back, dx], to),
+            )
+
+    opposite = (z + 4) % NZ
+    for t in range(NY):
+        (arrive_up if t % 2 == 0 else arrive_down)(t, 4)
+        if t < NY - 1:
+            attend(t + 1, NY - 1 - t, kv[t, opposite, 0], kv[t, opposite, 1], qt, m_ref, l_ref, acc_ref)
+        attend_same(t, opposite)
+        tile = slice(t * wide, (t + 1) * wide)
         total = l_ref[:, tile]
         some = total > 0.0
         safe = jnp.where(some, total, 1.0)
         o[t] = (acc_ref[:, tile] * (1.0 / safe)).T.astype(BF16)
         level = jnp.where(some, m_ref[:, tile] * (SCALE * LOG2E) + jnp.log2(safe), NEG)
         lse[t] = jnp.broadcast_to(level, (8, wide))
-        for dx in range(2):
-            if d or dx:
-                to, back = at(t, z, x + dx), (NY - d) % NY
-                copy = remote(
-                    o.at[t, q_rows(x + dx)], o_recv.at[y, x], o_send_sem.at[d, dx], o_recv_sem.at[back, dx], to
-                )
-                copy.start()
-                sent.append(copy)
-                copy = remote(lse.at[t], lse_recv.at[y, x], l_send_sem.at[d, dx], l_recv_sem.at[back, dx], to)
-                copy.start()
-                sent.append(copy)
+        for elsewhere, copies in tile_copies(t):
+
+            @pl.when(elsewhere)
+            def _():
+                for copy in copies:
+                    copy.start()
+
     o_recv[y, x] = o[y, q_rows(x), :]
     lse_recv[y, x] = lse[y]
 
@@ -524,6 +522,14 @@
     out[...] = total + share(diagonal)
     for d in (1, 2, 3):
         pair_copy((r + d) % GROUP).wait_send()
+    for t in range(NY):
+        for elsewhere, copies in tile_copies(t):
+
+            @pl.when(elsewhere)
+            def _():
+                for copy in copies:
+                    copy.wait_send()
+
     for copy in sent + exchange(1, t_buf, g, in_chain) + exchange(2, u_buf, y, in_column) + states_out():
         copy.wait_send()
     for j in range(NY):

time: 76.7 us -> 73.1 us (0.953); the launches traced: 75.2 us -> 73 us
  Pallas kernels: 73.5 us -> 71.2 us
    pallas_call x1, Pallas kernels: 73.5 us -> 71.2 us  [local(): pl.pallas_call(main_kernel, out_shape=struct((tokens, cols), F32), in_spe...]
where the time goes in v5:
time: 73.1 us; the launch traced here: 73 us
  Pallas kernels  71.2 us (97%)
  other arithmetic  1.71 us (2%)
    pallas_call x1, Pallas kernels, local(): pl.pallas_call(main_kernel, out_shape=struct((tokens, cols), F32), in_spe...  71.2 us
    convert_element_type x1, other arithmetic, local(): return (hidden_in.astype(F32) + shared).astype(BF16)  1.71 us

profile of v5, /device:TPU:25, one launch (start us, length us, event | category | flops | bytes accessed | tf_op | source)
XLA Modules:
  0.0 73.0 jit_solution(2014747522302714412)
XLA Ops:
  0.0 0.0 copy-start
  0.0 71.2 %shard_map.127 = f32[192,512]{1,0:T(8,128)} custom-call(bf16[192,512]{1,0:T(8,128)(2,1)} %dq_in.1, bf16[192,512]{1,0:T(8,128)(2,1)} %dk_in.1, bf16[192,512]{1,0:T(8,128)(2,1)} %dv_in.1, f32[4,192]{1,0:T(4,128)} %bitcast.5, f32[4,192]{1,0:T(4,128)} %bitcast.6, s32[1,192]{1,0:T(1,128)} %bitcast.7, bf16[192,512]{1,0:T(8,128)(2,1)} %aq.1, bf16[192,512]{1,0:T(8,128)(2,1)} %ak.1, ...), custom_call_target="tpu_custom_call" | custom-call | tf_op jit(solution)/shard_map/pallas_call | solution.py:557
  71.3 0.0 copy-done
  71.3 1.7 %add_convert_fusion = bf16[192,512]{1,0:T(8,128)(2,1)} fusion(f32[192,512]{1,0:T(8,128)} %shard_map.127, bf16[192,512]{1,0:T(8,128)(2,1)S(1)} %copy-done), kind=kLoop, calls=%fused_computation | loop fusion | flops 294912 | bytes 786432 | tf_op jit(solution)/shard_map/convert_element_type | solution.py:611
Async XLA Ops:
  0.0 71.3 %copy-start = (bf16[192,512]{1,0:T(8,128)(2,1)S(1)}, bf16[192,512]{1,0:T(8,128)(2,1)}, u32[]{:S(2)}) copy-start(bf16[192,512]{1,0:T(8,128)(2,1)} %param.13) | copy-start | bytes 589828

commit v6 on v5

--- a/solution.py
+++ b/solution.py
@@ -410,12 +410,13 @@
             pl.when(n == when)(stage)
         before, after = (z - hop + NZ) % NZ, (z + hop) % NZ
 
-        @pl.when(hop == 3)
+        @pl.when((n >= 6) & (n < 10))
         def _():
-            arrive_up(yk, 3)
-            pl.when(yk % 2 == 0)(lambda: upward(yk, 3).start())
-            arrive_down(yk, 3)
-            pl.when(yk % 2 == 1)(lambda: downward(yk, 3).start())
+            early = n - 6
+            arrive_up(early, 3)
+            pl.when(early % 2 == 0)(lambda: upward(early, 3).start())
+            arrive_down(early, 3)
+            pl.when(early % 2 == 1)(lambda: downward(early, 3).start())
 
         attend_later(
             yk,

time: 73.1 us -> 71.7 us (0.981)
  the two profiles are of different devices: /device:TPU:25 before, /device:TPU:31 now
where the time goes in v6:
time: 71.7 us; the launch traced here: 71.5 us
  Pallas kernels  69.8 us (97%)
  other arithmetic  1.71 us (2%)
    pallas_call x1, Pallas kernels, local(): pl.pallas_call(main_kernel, out_shape=struct((tokens, cols), F32), in_spe...  69.8 us
    convert_element_type x1, other arithmetic, local(): return (hidden_in.astype(F32) + shared).astype(BF16)  1.71 us

profile of v6, /device:TPU:31, one launch (start us, length us, event | category | flops | bytes accessed | tf_op | source)
XLA Modules:
  0.0 71.5 jit_solution(4623126082408200894)
XLA Ops:
  0.0 0.0 copy-start
  0.0 69.8 %shard_map.127 = f32[192,512]{1,0:T(8,128)} custom-call(bf16[192,512]{1,0:T(8,128)(2,1)} %dq_in.1, bf16[192,512]{1,0:T(8,128)(2,1)} %dk_in.1, bf16[192,512]{1,0:T(8,128)(2,1)} %dv_in.1, f32[4,192]{1,0:T(4,128)} %bitcast.5, f32[4,192]{1,0:T(4,128)} %bitcast.6, s32[1,192]{1,0:T(1,128)} %bitcast.7, bf16[192,512]{1,0:T(8,128)(2,1)} %aq.1, bf16[192,512]{1,0:T(8,128)(2,1)} %ak.1, ...), custom_call_target="tpu_custom_call" | custom-call | tf_op jit(solution)/shard_map/pallas_call | solution.py:558
  69.8 0.0 copy-done
  69.8 1.7 %add_convert_fusion = bf16[192,512]{1,0:T(8,128)(2,1)} fusion(f32[192,512]{1,0:T(8,128)} %shard_map.127, bf16[192,512]{1,0:T(8,128)(2,1)S(1)} %copy-done), kind=kLoop, calls=%fused_computation | loop fusion | flops 294912 | bytes 786432 | tf_op jit(solution)/shard_map/convert_element_type | solution.py:612
Async XLA Ops:
  0.0 69.8 %copy-start = (bf16[192,512]{1,0:T(8,128)(2,1)S(1)}, bf16[192,512]{1,0:T(8,128)(2,1)}, u32[]{:S(2)}) copy-start(bf16[192,512]{1,0:T(8,128)(2,1)} %param.13) | copy-start | bytes 589828

commit v7 on v6

--- a/solution.py
+++ b/solution.py
@@ -257,10 +257,10 @@
         return remote(ab_send.at[h], ab_recv.at[r], c_send.at[0, d], c_recv.at[0, d], of_group(h))
 
     for h in range(HEADS):
+        if h:
+            first_round(h)
         delta_head(h, dq, dk, dv, betas, cum_col, cum_row, oloc, qeff, ab_send)
         pl.when(r != h)(lambda: pair_copy(h).start())
-        if h:
-            first_round(h)
 
     def pairs_in():
         for d in (1, 2, 3):

time: 71.7 us -> 71.6 us (level)
  the two profiles are of different devices: /device:TPU:31 before, /device:TPU:25 now
where the time goes in v7:
time: 71.6 us; the launch traced here: 71.3 us
  Pallas kernels  69.6 us (97%)
  other arithmetic  1.71 us (2%)
    pallas_call x1, Pallas kernels, local(): pl.pallas_call(main_kernel, out_shape=struct((tokens, cols), F32), in_spe...  69.6 us
    convert_element_type x1, other arithmetic, local(): return (hidden_in.astype(F32) + shared).astype(BF16)  1.71 us

profile of v7, /device:TPU:25, one launch (start us, length us, event | category | flops | bytes accessed | tf_op | source)
XLA Modules:
  0.0 71.3 jit_solution(14083950767804468575)
XLA Ops:
  0.0 0.0 copy-start
  0.0 69.6 %shard_map.127 = f32[192,512]{1,0:T(8,128)} custom-call(bf16[192,512]{1,0:T(8,128)(2,1)} %dq_in.1, bf16[192,512]{1,0:T(8,128)(2,1)} %dk_in.1, bf16[192,512]{1,0:T(8,128)(2,1)} %dv_in.1, f32[4,192]{1,0:T(4,128)} %bitcast.5, f32[4,192]{1,0:T(4,128)} %bitcast.6, s32[1,192]{1,0:T(1,128)} %bitcast.7, bf16[192,512]{1,0:T(8,128)(2,1)} %aq.1, bf16[192,512]{1,0:T(8,128)(2,1)} %ak.1, ...), custom_call_target="tpu_custom_call" | custom-call | tf_op jit(solution)/shard_map/pallas_call | solution.py:558
  69.6 0.0 copy-done
  69.6 1.7 %add_convert_fusion = bf16[192,512]{1,0:T(8,128)(2,1)} fusion(f32[192,512]{1,0:T(8,128)} %shard_map.127, bf16[192,512]{1,0:T(8,128)(2,1)S(1)} %copy-done), kind=kLoop, calls=%fused_computation | loop fusion | flops 294912 | bytes 786432 | tf_op jit(solution)/shard_map/convert_element_type | solution.py:612
Async XLA Ops:
  0.0 69.6 %copy-start = (bf16[192,512]{1,0:T(8,128)(2,1)S(1)}, bf16[192,512]{1,0:T(8,128)(2,1)}, u32[]{:S(2)}) copy-start(bf16[192,512]{1,0:T(8,128)(2,1)} %param.13) | copy-start | bytes 589828
